TPU v7x, 32 devices: a whole 2x2x4 slice. The times are simulated.
32 devices in a mesh: branch: 4 (over y, x), crops: 8 (over z, core).
Axes of the slice: x: 2, y: 2, z: 4, core: 2. Of those that a mesh axis runs over, the one named last changes fastest.
Arguments:
- features: bfloat16 [4, 6144, 128], P('branch', 'crops'), may hold values from -16 to 16
- weights: bfloat16 [4, 2, 1708032], P('branch'), may hold values from -0.1875 to 0.1875
- gains: float32 [4, 2, 8, 256], P('branch'), may hold values from 0.1 to 1.9
- shifts: float32 [4, 2, 8, 256], P('branch'), may hold values from -3 to 3
- cotangent: bfloat16 [4, 6144, 128], P('branch', 'crops'), may hold values from -16 to 16
- size_group: int32 [8], replicated, may hold values from 0 to 1, as said below
Outputs:
- outputs: bfloat16 [4, 6144, 128], P('branch', 'crops')
- input_grad: float32 [4, 6144, 128], P('branch', 'crops')
- weight_grad: float32 [4, 2, 1708032], P('branch', None, 'crops')
- gain_grad: float32 [4, 2, 8, 256], P('branch', None, None, 'crops')
- shift_grad: float32 [4, 2, 8, 256], P('branch', None, None, 'crops')
Inputs may be any that keep to these rules, and one draw needn't show every extreme that they name: `size_group`: exactly 2 entries are 1; those devices hold large crops, the others small ones.
All inputs are finite; a program needn't handle non-finite values.
Results may differ from a plain program's by a relative error of at most 0.014.
Values may be sent and summed in bfloat16 or wider, within the bound.
A program may use at most 320 MiB of HBM per device.

v0:
```python
from functools import partial
from types import SimpleNamespace
import math

import jax
import jax.numpy as jnp
import numpy as np
from jax import lax
from jax.experimental import pallas as pl
from jax.experimental.layout import Layout, with_layout_constraint
from jax.experimental.pallas import tpu as pltpu
from jax.sharding import PartitionSpec as P

C0 = 32
BLOCKS = 1
MODULES = 2
CROPS_DEV = 1
SH = 32
SW = 24
LH = 64
LW = 48
ROWS = 768
MSG_ROWS = 384


EPS = 1e-05


def as_sent(x):

    def short(part):
        return part.astype(jnp.bfloat16) if part.dtype == jnp.float32 else part

    return jax.tree.map(short, x)


def sender_plan(branch_index, top_channels, blocks):
    channels = top_channels << branch_index
    operations = []
    for block_index in range(blocks):
        operations.append(
            SimpleNamespace(
                phase=2 * block_index,
                source=("h", block_index),
                level=branch_index,
                cin=channels,
                cout=channels,
                stride=1,
                taps=3,
                act="silu",
                output=("u", block_index),
                skip=None,
                dest=-1,
            )
        )
        operations.append(
            SimpleNamespace(
                phase=2 * block_index + 1,
                source=("u", block_index),
                level=branch_index,
                cin=channels,
                cout=channels,
                stride=1,
                taps=3,
                act="res",
                output=("h", block_index + 1),
                skip=("h", block_index),
                dest=-1,
            )
        )
    top_name = ("h", blocks)
    for target in range(branch_index):
        operations.append(
            SimpleNamespace(
                phase=2 * blocks,
                source=top_name,
                level=branch_index,
                cin=channels,
                cout=top_channels << target,
                stride=1,
                taps=1,
                act="none",
                output=None,
                skip=None,
                dest=target,
            )
        )
    for target in range(branch_index + 1, 4):
        for depth_step in range(1, target - branch_index + 1):
            is_last = depth_step == target - branch_index
            operations.append(
                SimpleNamespace(
                    phase=2 * blocks + depth_step - 1,
                    source=top_name if depth_step == 1 else ("chain", target, depth_step - 1),
                    level=branch_index + depth_step,
                    cin=channels,
                    cout=top_channels << target if is_last else channels,
                    stride=2,
                    taps=3,
                    act="none" if is_last else "silu",
                    output=None if is_last else ("chain", target, depth_step),
                    skip=None,
                    dest=target if is_last else -1,
                )
            )
    for position, operation in enumerate(operations):
        operation.slot = position
        operation.size = (
            operation.taps * operation.taps * operation.cin * operation.cout
        )
        if operation.taps == 1:
            operation.kshape = (operation.cin, operation.cout)
        else:
            operation.kshape = (3, 3, operation.cin, operation.cout)
    return operations


def phase_lengths(top_channels, blocks):
    phase_count = 2 * blocks + 3
    lengths = [0] * phase_count
    for branch_index in range(4):
        per_phase = [0] * phase_count
        for operation in sender_plan(branch_index, top_channels, blocks):
            per_phase[operation.phase] += operation.size
        lengths = [max(current, candidate) for current, candidate in zip(lengths, per_phase)]
    return lengths


def weighted_plan(branch_index, top_channels, blocks):
    lengths = phase_lengths(top_channels, blocks)
    starts = [sum(lengths[:phase_index]) for phase_index in range(len(lengths))]
    running = [0] * len(lengths)
    operations = sender_plan(branch_index, top_channels, blocks)
    for operation in operations:
        phase_index = operation.phase
        operation.inner = running[phase_index]
        operation.offset = starts[phase_index] + running[phase_index]
        operation.position = sum(
            (1 for earlier in operations[: operation.slot] if earlier.phase == phase_index)
        )
        running[phase_index] += operation.size
    return operations


def phase_operations(branch_index, phase_index):
    return [
        operation
        for operation in weighted_plan(branch_index, C0, BLOCKS)
        if operation.phase == phase_index
    ]


def input_names(operations):
    source_names = []
    for operation in operations:
        if operation.source not in source_names:
            source_names.append(operation.source)
    return source_names


def silu_slope(value):
    sigmoid = jax.nn.sigmoid(value)
    return sigmoid * (1.0 + value * (1.0 - sigmoid))


def crop_cells(size_kind):
    return (LH, LW) if size_kind else (SH, SW)


def map_dims(size_kind, level, channels):
    height, breadth = crop_cells(size_kind)
    return (CROPS_DEV, height >> level, breadth >> level, channels)


def source_dims(branch_index, size_kind, map_name):
    level = branch_index + map_name[2] if map_name[0] == "chain" else branch_index
    return map_dims(size_kind, level, C0 << branch_index)


def preact_dims(size_kind, operation):
    return map_dims(size_kind, operation.level, operation.cout)


def to_canvas(arrays, value_type):
    if not arrays:
        return jnp.zeros((ROWS, 128), value_type)
    flattened = jnp.concatenate([array.reshape(-1).astype(value_type) for array in arrays])
    return jnp.pad(flattened, (0, ROWS * 128 - flattened.shape[0])).reshape(ROWS, 128)


def from_canvas(canvas, dims_list):
    flattened = canvas.reshape(-1)
    pieces = []
    offset = 0
    for dims_entry in dims_list:
        count_here = math.prod(dims_entry)
        pieces.append(flattened[offset : offset + count_here].reshape(dims_entry))
        offset += count_here
    return pieces


def to_slot(array):
    flattened = array.reshape(-1)
    return jnp.pad(flattened, (0, MSG_ROWS * 128 - flattened.shape[0])).reshape(MSG_ROWS, 128)


def from_slot(slot_rows, dims_entry):
    return slot_rows.reshape(-1)[: math.prod(dims_entry)].reshape(dims_entry)


def upsample(message, factor):
    crop_count, height, breadth, channels = message.shape
    widened = jnp.broadcast_to(
        message[:, :, None, :, None, :], (crop_count, height, factor, breadth, factor, channels)
    )
    return widened.reshape(crop_count, height * factor, breadth * factor, channels)


def block_pool(array, factor):
    crop_count, height, breadth, channels = array.shape
    return array.reshape(
        crop_count, height // factor, factor, breadth // factor, factor, channels
    ).sum(axis=(2, 4))


def kernel_piece(module_weights, operation):
    start = operation.offset
    return module_weights[start : start + operation.size].reshape(operation.kshape)


def conv_forward(operation, source, kernel):
    if operation.taps == 1:
        return jnp.einsum("nhwc,cd->nhwd", source, kernel, preferred_element_type=jnp.float32)
    stride = operation.stride
    return lax.conv_general_dilated(
        source,
        kernel,
        (stride, stride),
        ((1, 1), (1, 1)),
        dimension_numbers=("NHWC", "HWIO", "NHWC"),
        preferred_element_type=jnp.float32,
    )


def conv_backward(operation, source, kernel, upstream):
    if operation.taps == 1:
        source_grad = jnp.einsum(
            "nhwd,cd->nhwc", upstream, kernel, preferred_element_type=jnp.float32
        )
        kernel_grad = jnp.einsum(
            "nhwc,nhwd->cd", source, upstream, preferred_element_type=jnp.float32
        )
        return (source_grad, kernel_grad)
    stride = operation.stride
    flipped = jnp.transpose(kernel[::-1, ::-1], (0, 1, 3, 2))
    high_pad = 2 if stride == 2 else 1
    source_grad = lax.conv_general_dilated(
        upstream,
        flipped,
        (1, 1),
        ((1, high_pad), (1, high_pad)),
        lhs_dilation=(stride, stride),
        dimension_numbers=("NHWC", "HWIO", "NHWC"),
        preferred_element_type=jnp.float32,
    )
    kernel_grad = lax.conv_general_dilated(
        source,
        upstream,
        (1, 1),
        ((1, 2 - stride), (1, 2 - stride)),
        rhs_dilation=(stride, stride),
        dimension_numbers=("CHWN", "IHWO", "NHWC"),
        preferred_element_type=jnp.float32,
    )
    return (source_grad, jnp.transpose(kernel_grad, (1, 2, 0, 3)))


def cell_total(counts, size_kind, level):
    height, breadth = crop_cells(size_kind)
    return counts[size_kind] * float(CROPS_DEV * (height >> level) * (breadth >> level))


def norm_terms(totals, counts, size_kind, operation):
    cells_here = cell_total(counts, size_kind, operation.level)
    channels = operation.cout
    position = operation.position
    average = totals[size_kind, 0, position, :channels] / cells_here
    variance = totals[size_kind, 1, position, :channels] / cells_here - average * average
    return (average, lax.rsqrt(variance + EPS))


def forward_conv(branch_index, size_kind, phase_index, source_canvas, module_weights):
    operations = phase_operations(branch_index, phase_index)
    source_names = input_names(operations)
    pieces = from_canvas(
        source_canvas, [source_dims(branch_index, size_kind, map_name) for map_name in source_names]
    )
    sources = {
        map_name: piece.astype(jnp.bfloat16) for map_name, piece in zip(source_names, pieces)
    }
    preacts = []
    totals = jnp.zeros((2, 2, 3, 8 * C0), jnp.float32)
    for operation in operations:
        preact = conv_forward(
            operation, sources[operation.source], kernel_piece(module_weights, operation)
        )
        preacts.append(preact)
        channels = operation.cout
        position = operation.position
        totals = totals.at[size_kind, 0, position, :channels].set(jnp.sum(preact, axis=(0, 1, 2)))
        totals = totals.at[size_kind, 1, position, :channels].set(
            jnp.sum(preact * preact, axis=(0, 1, 2))
        )
    return (to_canvas(preacts, jnp.float32), totals)


def forward_norm(
    branch_index,
    size_kind,
    phase_index,
    preact_canvas,
    totals,
    counts,
    module_gains,
    module_shifts,
    skip_canvas,
    message_buffer,
):
    operations = phase_operations(branch_index, phase_index)
    preacts = from_canvas(
        preact_canvas, [preact_dims(size_kind, operation) for operation in operations]
    )
    skip_map = from_canvas(skip_canvas, [map_dims(size_kind, branch_index, C0 << branch_index)])[0]
    produced = []
    for operation, preact in zip(operations, preacts):
        average, inverse_std = norm_terms(totals, counts, size_kind, operation)
        norm_slot = operation.slot
        channels = operation.cout
        normed = (preact - average) * inverse_std * module_gains[
            norm_slot, :channels
        ] + module_shifts[norm_slot, :channels]
        if operation.act == "silu":
            produced.append(jax.nn.silu(normed))
        elif operation.act == "res":
            produced.append(jax.nn.silu(normed + skip_map))
        else:
            message_buffer = message_buffer.at[operation.dest].set(
                to_slot(normed.astype(jnp.bfloat16))
            )
    return (to_canvas(produced, jnp.float32), message_buffer)


def receive_forward(branch_index, size_kind, top_canvas, received):
    channels = C0 << branch_index
    summed = from_canvas(top_canvas, [map_dims(size_kind, branch_index, channels)])[0]
    for sender in range(4):
        if sender < branch_index:
            summed = summed + from_slot(
                received[sender], map_dims(size_kind, branch_index, channels)
            ).astype(jnp.float32)
        elif sender > branch_index:
            coarse = from_slot(received[sender], map_dims(size_kind, sender, channels))
            summed = summed + upsample(coarse, 2 ** (sender - branch_index)).astype(jnp.float32)
    return (to_canvas([jax.nn.silu(summed)], jnp.float32), to_canvas([summed], jnp.float32))


def receive_backward(branch_index, size_kind, grad_canvas, summed_canvas):
    dims_here = map_dims(size_kind, branch_index, C0 << branch_index)
    upstream = from_canvas(grad_canvas, [dims_here])[0]
    summed = from_canvas(summed_canvas, [dims_here])[0]
    summed_grad = upstream * silu_slope(summed)
    buffer = jnp.zeros((4, MSG_ROWS, 128), jnp.bfloat16)
    for sender in range(4):
        if sender < branch_index:
            buffer = buffer.at[sender].set(to_slot(summed_grad.astype(jnp.bfloat16)))
        elif sender > branch_index:
            pooled = block_pool(summed_grad, 2 ** (sender - branch_index))
            buffer = buffer.at[sender].set(to_slot(pooled.astype(jnp.bfloat16)))
    return (to_canvas([summed_grad], jnp.float32), buffer)


def backward_stats(
    branch_index,
    size_kind,
    phase_index,
    dout_canvas,
    message_grads,
    preact_canvas,
    totals,
    counts,
    module_gains,
    module_shifts,
    skip_canvas,
):
    operations = phase_operations(branch_index, phase_index)
    preacts = from_canvas(
        preact_canvas, [preact_dims(size_kind, operation) for operation in operations]
    )
    producing = [operation for operation in operations if operation.act != "none"]
    output_grads = from_canvas(
        dout_canvas, [preact_dims(size_kind, operation) for operation in producing]
    )
    grads_by_name = {
        operation.output: piece for operation, piece in zip(producing, output_grads)
    }
    skip_map = from_canvas(skip_canvas, [map_dims(size_kind, branch_index, C0 << branch_index)])[0]
    upstreams = []
    skip_grads = []
    sums_local = jnp.zeros((2, 2, 3, 8 * C0), jnp.float32)
    for operation, preact in zip(operations, preacts):
        average, inverse_std = norm_terms(totals, counts, size_kind, operation)
        norm_slot = operation.slot
        channels = operation.cout
        centered = (preact - average) * inverse_std
        normed = centered * module_gains[norm_slot, :channels] + module_shifts[norm_slot, :channels]
        if operation.act == "silu":
            upstream = grads_by_name[operation.output] * silu_slope(normed)
        elif operation.act == "res":
            upstream = grads_by_name[operation.output] * silu_slope(normed + skip_map)
            skip_grads.append(upstream)
        else:
            upstream = from_slot(
                message_grads[operation.dest], preact_dims(size_kind, operation)
            ).astype(jnp.float32)
        upstreams.append(upstream)
        position = operation.position
        sums_local = sums_local.at[size_kind, 0, position, :channels].set(
            jnp.sum(upstream, axis=(0, 1, 2))
        )
        sums_local = sums_local.at[size_kind, 1, position, :channels].set(
            jnp.sum(upstream * centered, axis=(0, 1, 2))
        )
    return (to_canvas(upstreams, jnp.float32), sums_local, to_canvas(skip_grads, jnp.float32))


def backward_apply(
    branch_index,
    size_kind,
    phase_index,
    upstream_canvas,
    preact_canvas,
    totals,
    grad_totals,
    counts,
    source_canvas,
    module_weights,
    module_gains,
):
    operations = phase_operations(branch_index, phase_index)
    preacts = from_canvas(
        preact_canvas, [preact_dims(size_kind, operation) for operation in operations]
    )
    upstreams = from_canvas(
        upstream_canvas, [preact_dims(size_kind, operation) for operation in operations]
    )
    source_names = input_names(operations)
    source_list = [source_dims(branch_index, size_kind, map_name) for map_name in source_names]
    pieces = from_canvas(source_canvas, source_list)
    sources = {
        map_name: piece.astype(jnp.bfloat16) for map_name, piece in zip(source_names, pieces)
    }
    source_grads = {
        map_name: jnp.zeros(dims_entry, jnp.float32)
        for map_name, dims_entry in zip(source_names, source_list)
    }
    kernel_grads = []
    slot_count = module_gains.shape[0]
    gain_part = jnp.zeros((slot_count, 8 * C0), jnp.float32)
    shift_part = jnp.zeros((slot_count, 8 * C0), jnp.float32)
    for operation, preact, upstream in zip(operations, preacts, upstreams):
        average, inverse_std = norm_terms(totals, counts, size_kind, operation)
        cells_here = cell_total(counts, size_kind, operation.level)
        norm_slot = operation.slot
        channels = operation.cout
        position = operation.position
        centered = (preact - average) * inverse_std
        mean_upstream = grad_totals[size_kind, 0, position, :channels] / cells_here
        mean_cross = grad_totals[size_kind, 1, position, :channels] / cells_here
        preact_grad = (
            module_gains[norm_slot, :channels]
            * inverse_std
            * (upstream - mean_upstream - centered * mean_cross)
        )
        source_grad, kernel_grad = conv_backward(
            operation,
            sources[operation.source],
            kernel_piece(module_weights, operation),
            preact_grad.astype(jnp.bfloat16),
        )
        source_grads[operation.source] = source_grads[operation.source] + source_grad
        kernel_grads.append(kernel_grad.reshape(-1))
        gain_part = gain_part.at[norm_slot, :channels].set(
            grad_totals[0, 1, position, :channels] + grad_totals[1, 1, position, :channels]
        )
        shift_part = shift_part.at[norm_slot, :channels].set(
            grad_totals[0, 0, position, :channels] + grad_totals[1, 0, position, :channels]
        )
    phase_length = phase_lengths(C0, BLOCKS)[phase_index]
    if kernel_grads:
        joined = jnp.concatenate(kernel_grads)
        weight_part = jnp.pad(joined, (0, phase_length - joined.shape[0]))
    else:
        weight_part = jnp.zeros((phase_length,), jnp.float32)
    return (
        to_canvas([source_grads[map_name] for map_name in source_names], jnp.float32),
        weight_part,
        gain_part,
        shift_part,
    )


def on_device(features, weights, gains, shifts, cotangent, size_group):
    crop_shard = lax.axis_index("crops")
    shard_count = lax.axis_size("crops")
    crop_kind = size_group[crop_shard]
    large_count = jnp.sum(size_group).astype(jnp.float32)
    counts = jnp.stack([shard_count - large_count, large_count])
    case_index = lax.axis_index("branch") * 2 + crop_kind
    phase_total = 2 * BLOCKS + 3
    zero_canvas = jnp.zeros((ROWS, 128), jnp.float32)
    empty_buffer = jnp.zeros((4, MSG_ROWS, 128), jnp.bfloat16)

    def run_phase(function, statics, operands):
        branches_list = [
            partial(function, branch_index, size_kind, *statics)
            for branch_index in range(4)
            for size_kind in range(2)
        ]
        return lax.switch(case_index, branches_list, *operands)

    def statistics(local_totals):
        return lax.psum(local_totals, "crops")

    def module_forward(module, start_canvas, kept):
        module_weights = weights[0, module]
        module_gains = gains[0, module]
        module_shifts = shifts[0, module]
        record = SimpleNamespace(sources=[], preacts=[], totals=[])
        h_canvas = start_canvas
        u_canvas = zero_canvas
        chain_canvas = zero_canvas
        buffer = empty_buffer
        for phase_index in range(phase_total):
            if phase_index < 2 * BLOCKS:
                source = h_canvas if phase_index % 2 == 0 else u_canvas
            elif phase_index == 2 * BLOCKS:
                source = h_canvas
            else:
                source = chain_canvas
            preact, local_totals = run_phase(forward_conv, (phase_index,), (source, module_weights))
            global_totals = kept.totals[phase_index] if kept else statistics(local_totals)
            produced, buffer = run_phase(
                forward_norm,
                (phase_index,),
                (preact, global_totals, counts, module_gains, module_shifts, h_canvas, buffer),
            )
            record.sources.append(source)
            record.preacts.append(preact)
            record.totals.append(global_totals)
            if phase_index < 2 * BLOCKS:
                if phase_index % 2 == 0:
                    u_canvas = produced
                else:
                    h_canvas = produced
            else:
                chain_canvas = produced
        received = (
            kept.received
            if kept
            else jax.tree.map(
                lambda part, own: part.astype(own.dtype),
                lax.all_to_all(as_sent(buffer), "branch", split_axis=0, concat_axis=0, tiled=True),
                buffer,
            )
        )
        result, summed = run_phase(receive_forward, (), (h_canvas, received))
        record.summed = summed
        record.received = received
        return (result, record)

    checkpoints = [features[0].astype(jnp.float32)]
    first_records = []
    for module in range(MODULES):
        result, record = module_forward(module, checkpoints[-1], None)
        checkpoints.append(result)
        first_records.append(record)
    outputs = checkpoints[-1].astype(jnp.bfloat16)
    grad_canvas = cotangent[0].astype(jnp.float32)
    module_grads = [None] * MODULES
    gain_grads = [None] * MODULES
    shift_grads = [None] * MODULES
    for module in reversed(range(MODULES)):
        kept = None
        unused_result, record = module_forward(module, checkpoints[module], kept)
        module_module_weights = weights[0, module]
        module_module_gains = gains[0, module]
        module_module_shifts = shifts[0, module]
        summed_grad, back_buffer = run_phase(receive_backward, (), (grad_canvas, record.summed))
        message_grads = jax.tree.map(
            lambda part, own: part.astype(own.dtype),
            lax.all_to_all(as_sent(back_buffer), "branch", split_axis=0, concat_axis=0, tiled=True),
            back_buffer,
        )
        top_grad = summed_grad
        chain_grad = zero_canvas
        u_grad = zero_canvas
        pending_skip = zero_canvas
        weight_parts = [None] * phase_total
        gain_total = jnp.zeros(gains.shape[2:], jnp.float32)
        shift_total = jnp.zeros(gains.shape[2:], jnp.float32)
        for module_phase_index in reversed(range(phase_total)):
            if module_phase_index >= 2 * BLOCKS:
                output_grad = chain_grad
                skip_canvas = zero_canvas
            elif module_phase_index % 2 == 1:
                output_grad = top_grad
                skip_canvas = record.sources[module_phase_index - 1]
            else:
                output_grad = u_grad
                skip_canvas = zero_canvas
            module_preact = record.preacts[module_phase_index]
            totals = record.totals[module_phase_index]
            upstream, module_local_totals, skip_grad = run_phase(
                backward_stats,
                (module_phase_index,),
                (
                    output_grad,
                    message_grads,
                    module_preact,
                    totals,
                    counts,
                    module_module_gains,
                    module_module_shifts,
                    skip_canvas,
                ),
            )
            grad_totals = lax.psum(module_local_totals, "crops")
            source_grad, weight_parts[module_phase_index], gain_part, shift_part = run_phase(
                backward_apply,
                (module_phase_index,),
                (
                    upstream,
                    module_preact,
                    totals,
                    grad_totals,
                    counts,
                    record.sources[module_phase_index],
                    module_module_weights,
                    module_module_gains,
                ),
            )
            gain_total = gain_total + gain_part
            shift_total = shift_total + shift_part
            if module_phase_index > 2 * BLOCKS:
                chain_grad = source_grad
            elif module_phase_index == 2 * BLOCKS:
                top_grad = top_grad + source_grad
            elif module_phase_index % 2 == 1:
                u_grad = source_grad
                pending_skip = skip_grad
            else:
                top_grad = source_grad + pending_skip
        joined = jnp.concatenate(weight_parts)
        weight_grad = jnp.pad(joined, (0, weights.shape[2] - joined.shape[0]))
        grad_canvas, weight_grad, gain_grads[module], shift_grads[module] = (
            top_grad,
            weight_grad,
            gain_total,
            shift_total,
        )
        module_grads[module] = weight_grad
    weight_out = lax.psum_scatter(jnp.stack(module_grads), "crops", scatter_dimension=1, tiled=True)
    share = gains.shape[3] // shard_count
    gain_out = lax.dynamic_slice_in_dim(jnp.stack(gain_grads), crop_shard * share, share, axis=2)
    shift_out = lax.dynamic_slice_in_dim(jnp.stack(shift_grads), crop_shard * share, share, axis=2)
    return (outputs[None], grad_canvas[None], weight_out[None], gain_out[None], shift_out[None])


LANES = 128
SLOTS = 8
MASKS = 7
DOWN = (((1,), (0,)), ((), ()))
ACROSS = (((1,), (1,)), ((), ()))
ALONG = (((0,), (0,)), ((), ()))


def unit_table(k):
    operations = weighted_plan(k, C0, BLOCKS)
    planes = 8 >> k
    channels = C0 << k
    units = {}
    stat = 0

    def add(name, kind, source, lanes_in, planes_in, planes_out, members):
        nonlocal stat
        segs = []
        tile = 0
        for operation, lanes, chain in members:
            cout = operation.cout
            level = operation.level if operation.taps == 3 else operation.dest
            segs.append(
                SimpleNamespace(
                    slot=operation.slot,
                    off=operation.offset // LANES,
                    cin=operation.cin,
                    cout=cout,
                    taps=operation.taps,
                    tile=tile,
                    tiles=lanes // LANES,
                    blocks=max(1, (8 >> level)),
                    dest=operation.dest,
                    act=operation.act,
                    chain=chain,
                    up=k - operation.dest if operation.taps == 1 else 0,
                )
            )
            tile += lanes // LANES
        rows = {"s1": (384, 384, 512, 768)[k], "s2": lanes_in + LANES, "p1": 256}[kind]
        units[name] = SimpleNamespace(
            name=name,
            kind=kind,
            source=source,
            lanes_in=lanes_in,
            blocks_in=planes_in,
            planes_in=planes_in,
            planes=planes_out,
            segs=segs,
            tiles=tile,
            rows=rows,
            stat=stat,
            depth=1 if kind == "p1" else 3,
        )
        stat += tile

    add("a", "s1", "h", 256, planes, planes, [(operations[0], 256, None)])
    add("b", "s1", "u", 256, planes, planes, [(operations[1], 256, None)])
    ups = [operation for operation in operations if operation.taps == 1]
    if ups:
        add("u", "p1", "t", 256, planes, planes, [(operation, 256, None) for operation in ups])
    firsts, chains = [], {}
    for target in range(k + 1, 4):
        steps = [
            operation
            for operation in operations
            if operation.taps == 3 and operation.stride == 2
        ]
        start = sum(i - k for i in range(k + 1, target))
        chains[target] = steps[start : start + target - k]
        if target == k + 1:
            firsts.append((chains[target][0], 256, None))
        else:
            firsts.append((chains[target][0], LANES, "c1" if target == k + 2 else "c2"))
    if firsts:
        add("d", "s2", "t", 256, planes, planes // 2, firsts)
    if k <= 1:
        add("e", "s2", "c1", LANES, planes // 2, planes // 4, [(chains[k + 2][1], 256, None)])
    if k == 0:
        add("f", "s2", "c2", LANES, planes // 2, planes // 4, [(chains[3][1], LANES, "c3")])
        add("g", "s2", "c3", LANES, planes // 4, planes // 8, [(chains[3][2], 256, None)])
    return units


def links(k, unit, seg):
    cin = seg.cin
    count_in, count_out = unit.blocks_in, seg.blocks
    found = []
    if unit.kind == "p1":
        for plane in range(count_in):
            wide = 1 << seg.up
            found.append((plane * cin, 0, set(range(plane * wide, plane * wide + wide))))
        return found
    if unit.kind == "s1" and k == 3:
        return [(256 * tap, tap, {0}) for tap in range(3)]
    stride = 1 if unit.kind == "s1" else 2
    for plane in range(count_in):
        for tap in range(3):
            at = plane - tap + 1
            if at % stride == 0 and 0 <= at // stride < count_out:
                found.append((plane * cin, tap, {at // stride}))
    if stride == 1:
        found.append((256, 2, {count_out - 1}))
        found.append((unit.rows - cin, 0, {0}))
    else:
        lanes_in = unit.lanes_in
        found.append((lanes_in + (count_in - 1) * cin - (lanes_in - LANES), 0, {0}))
    return found


def message_slot(k, other):
    return sum(2 * (8 >> max(k, before)) for before in range(other) if before != k)


def log2(value):
    return value.bit_length() - 1


def sigmoid_of(value):
    return 0.5 * jnp.tanh(0.5 * value) + 0.5


def silu_of(value):
    return value * sigmoid_of(value)


def slope_of(value):
    sigmoid = sigmoid_of(value)
    return sigmoid * (1.0 + value * (1.0 - sigmoid))


def planes_loop(count, body, turns=1):
    def step(index, carry):
        for turn in range(turns):
            body(index * turns + turn)
        return carry

    turns = min(turns, count)
    if count == turns:
        for index in range(count):
            body(index)
    else:
        lax.fori_loop(0, count // turns, step, 0)


def planes_sum(count, body, initial, turns=1):
    def step(index, carry):
        for turn in range(turns):
            carry = body(index * turns + turn, carry)
        return carry

    turns = min(turns, count)
    if count == turns:
        return step(0, initial)
    return lax.fori_loop(0, count // turns, step, initial)


def partial_sum(value):
    rows = value.shape[0]
    return jnp.sum(value.reshape(rows // 8, 8, value.shape[1]), axis=0)


class Planes:
    def __init__(self, mode, tiles, planes, masks, rows, main, edge=None, right=None, narrow=False):
        self.narrow, self.pending = narrow, {}
        self.mode, self.tiles, self.planes = mode, tiles, planes
        self.masks, self.rows = masks, rows
        self.main, self.edge, self.right = main, edge, right
        self.base = 1 if mode in ("s1", "wide", "s2") else 0
        extra = {"s1": 2, "wide": 2, "s2": 1, "dz2": 1, "p": 0}[mode]
        self.span = planes + extra
        self.unit = tiles * self.span

    def at(self, m, tile, plane):
        return m * self.unit + tile * self.span + plane + self.base

    def edge_at(self, m, tile, plane):
        if self.mode == "s2" or self.narrow:
            return m * self.span + plane + self.base
        return self.at(m, tile, plane)

    def from_left(self, value):
        return pltpu.roll(value, 1, 0) * self.masks[1]

    def from_right(self, value):
        return pltpu.roll(value, self.rows - 1, 0) * self.masks[2]

    def store(self, m, tile, plane, value):
        self.put(m, tile, plane, value)
        if isinstance(plane, int):
            if plane == self.planes - 1:
                self.put_above(m, tile, value)
            if plane == 0:
                self.put_below(m, tile, value)

    def put(self, m, tile, plane, value):
        where = self.at(m, tile, plane)
        self.main[where] = value.astype(jnp.bfloat16)
        if self.mode == "s1":
            side = self.from_right(value) if tile == 0 else self.from_left(value)
            if not self.narrow:
                self.edge[where] = side.astype(jnp.bfloat16)
            elif tile == 0:
                self.pending[plane if isinstance(plane, int) else self.span] = side
            else:
                lane = lax.broadcasted_iota(jnp.int32, side.shape, 1)
                other = self.pending.pop(plane if isinstance(plane, int) else self.span)
                side = jnp.where(lane < LANES // 2, other, side)
                self.edge[self.edge_at(m, tile, plane)] = side.astype(jnp.bfloat16)
        elif self.mode == "wide":
            self.edge[where] = self.from_left(value).astype(jnp.bfloat16)
            self.right[where] = self.from_right(value).astype(jnp.bfloat16)
        elif self.mode == "s2":
            if tile == self.tiles - 1:
                self.edge[self.edge_at(m, tile, plane)] = self.from_left(value).astype(jnp.bfloat16)
        elif self.mode == "dz2":
            self.edge[where] = self.from_right(value).astype(jnp.bfloat16)

    def put_above(self, m, tile, last):
        if self.mode in ("s1", "wide", "s2"):
            above = pltpu.roll(last, 6, 0) * self.masks[3] + pltpu.roll(last, 3, 0) * self.masks[4]
            self.put(m, tile, -1, above)

    def put_below(self, m, tile, first):
        if self.mode in ("s1", "wide", "dz2"):
            rows = self.rows
            below = (
                pltpu.roll(first, rows - 6, 0) * self.masks[5]
                + pltpu.roll(first, rows - 3, 0) * self.masks[6]
            )
            self.put(m, tile, self.planes, below)

    def close(self, m):
        for tile in range(self.tiles):
            last = self.main[self.at(m, tile, self.planes - 1)].astype(jnp.float32)
            self.put_above(m, tile, last)
        for tile in range(self.tiles):
            first = self.main[self.at(m, tile, 0)].astype(jnp.float32)
            self.put_below(m, tile, first)


class Branch:
    def __init__(self, k, rows, large, small, share, refs, masks, core):
        self.k, self.rows, self.refs, self.masks = k, rows, refs, masks
        self.units = unit_table(k)
        self.planes = 8 >> k
        self.core = core
        self.large, self.small, self.count = large, small, large + small
        self.cells = (small * (SH // 8) * (SW // 8), large * (LH // 8) * (LW // 8))
        self.quarter = lax.axis_index("crops") // 2
        self.share = share
        r = refs
        make = partial(Planes, masks=masks, rows=rows)
        make_one = partial(make, narrow=k <= 1)
        one = "wide" if k == 3 else "s1"
        self.maps = dict(
            h=make_one(one, 2, self.planes, main=r.hC, edge=r.hE, right=r.hR),
            u=make_one(one, 2, self.planes, main=r.uC, edge=r.uE, right=r.uR),
            t=make("p" if k == 3 else "s2", 2, self.planes, main=r.tC, edge=r.tE),
        )
        if k <= 1:
            self.maps["c1"] = make("s2", 1, self.planes // 2, main=r.c1C, edge=r.c1E)
        if k == 0:
            self.maps["c2"] = make("s2", 1, 4, main=r.c2C, edge=r.c2E)
            self.maps["c3"] = make("s2", 1, 2, main=r.c3C, edge=r.c3E)
        self.grads = dict(t=r.gt, u=r.gu, c1=r.gc1, c2=r.gc2, c3=r.gc3)

    def lane_block(self, shape, cout):
        lanes = lax.broadcasted_iota(jnp.int32, shape, 1)
        return lanes >> log2(cout)

    def keep(self, value, cout, which):
        count = LANES // cout
        if len(which) == count:
            return value
        block = self.lane_block(value.shape, cout)
        mask = block == which[0]
        for entry in which[1:]:
            mask = mask | (block == entry)
        return jnp.where(mask, value, 0.0)

    def spread(self, value, cout):
        shift = LANES // 2
        while shift >= cout:
            value = value + pltpu.roll(value, shift, 1)
            shift //= 2
        return value

    def local_blocks(self, seg, tile, wanted):
        count = LANES // seg.cout
        return [q for q in range(count) if (tile * count + q) % seg.blocks in wanted]


    def segments(self):
        return [(unit, seg) for unit in self.units.values() for seg in unit.segs]

    def pieces(self):
        found, place = [], 0
        for index, (unit, seg) in enumerate(self.segments()):
            count = 2 * seg.taps**2 * seg.cin * seg.cout // LANES
            if self.k < 3:
                found.append((index, 0, count, place, index))
                place += count
            else:
                for d in range(unit.depth):
                    slot = len(found) % 3
                    found.append((index, d, count // unit.depth, slot * 3072, slot))
        return found

    def fetch(self, at):
        r = self.refs
        index, d, count, place, sem = self.pieces()[at]
        _, seg = self.segments()[index]
        return pltpu.make_async_copy(
            r.w.at[pl.ds(2 * seg.off + d * count, count)],
            r.raw.at[pl.ds(place, count)],
            r.wsem.at[sem],
        )

    def fetch_first(self):
        for at in range(len(self.pieces()) if self.k < 3 else 3):
            self.fetch(at).start()

    def expand(self, index):
        unit, seg = self.segments()[index]
        pieces = self.pieces()
        mine = [at for at, piece in enumerate(pieces) if piece[0] == index]
        if self.k < 3:
            (at,) = mine
            self.fetch(at).wait()
            count = pieces[at][2] // unit.depth
            planes_loop(
                unit.depth,
                lambda d: self.expand_row(unit, seg, d, count, pieces[at][3] + d * count),
            )
        else:
            for d, at in enumerate(mine):
                self.fetch(at).wait()
                self.expand_row(unit, seg, d, pieces[at][2], pieces[at][3])
                if at + 3 < len(pieces):
                    self.fetch(at + 3).start()
        for m in range(MODULES):
            self.spread_tables(m, unit, seg)

    def expand_row(self, unit, seg, d, count, place):
        r = self.refs
        chunk = math.gcd(count, 384)
        wf, rep = r.work, r.rep

        def widen(step):
            at = pl.multiple_of(step * chunk, 16)
            value = r.raw[pl.ds(pl.multiple_of(place + at, 16), chunk)].astype(jnp.float32)
            wf[pl.ds(at, chunk)] = value

        planes_loop(count // chunk, widen)
        count = count // MODULES
        depth, cin, cout = unit.depth, seg.cin, seg.cout
        target = getattr(r, "T" + unit.name)
        twice = unit.kind == "s1" and self.k < 3
        across = getattr(r, "T" + unit.name + unit.name) if twice else None
        by_row = {}
        for row, tap, wanted in links(self.k, unit, seg):
            by_row.setdefault(row, []).append((tap, wanted))

        def module(m):
            if cout < LANES:
                ratio = LANES // cout
                flat = wf[pl.ds(m, count, stride=2)]
                for part in range(ratio):
                    rep[pl.ds(part, count, stride=ratio)] = self.spread(
                        self.keep(flat, cout, [part]), cout
                    )

            def tap_rows(tap, tile):
                if cout < LANES:
                    return rep[tap * cin : (tap + 1) * cin]
                if cout == LANES:
                    return wf[pl.ds(m + tap * (2 * cin), cin, stride=2)]
                return wf[pl.ds(m + tap * (4 * cin) + 2 * tile, cin, stride=4)]

            def place(goal, taps_at, width, column, tile):
                made = {}
                for row in range(0, unit.rows, cin):
                    key = []
                    for tap, wanted in by_row.get(row, []):
                        local = self.local_blocks(seg, tile, wanted) if width <= LANES else [0]
                        if local:
                            key.append((tap, tuple(local)))
                    key = tuple(key)
                    if key not in made:
                        total = None
                        for tap, local in key:
                            piece = taps_at[tap]
                            if width <= LANES:
                                piece = self.keep(piece, width, local)
                            total = piece if total is None else total + piece
                        if total is None:
                            total = jnp.zeros((cin, LANES), jnp.float32)
                        made[key] = total.astype(jnp.bfloat16)
                    goal[m * depth + d, row : row + cin, column : column + LANES] = made[key]

            width = 3 if seg.taps == 3 else 1
            for tile in range(seg.tiles):
                if tile == 0 or cout > LANES:
                    taps_at = [tap_rows(tap, tile) for tap in range(width)]
                place(target, taps_at, cout, (seg.tile + tile) * LANES, tile)
            if not twice:
                return
            turned = []
            if cin == LANES:
                turned = [jnp.transpose(tap_rows(tap, 0)) for tap in range(3)]
            else:
                both = jnp.transpose(rep[0 : -(-3 * cin // LANES) * LANES])
                for tap in range(3):
                    first = tap * cin // LANES * LANES
                    value = both[0:cin, first : first + LANES]
                    value = self.keep(value, cin, [tap * cin % LANES // cin])
                    turned.append(self.spread(value, cin))
            for tile in range(2):
                place(across, turned[::-1], cin, tile * LANES, tile)

        planes_loop(MODULES, module)


    def parts(self, unit, source):
        if unit.kind == "p1":
            return [(source.main, range(2), source.at)]
        if source.mode == "wide":
            return [
                (source.edge, range(2), source.at),
                (source.main, range(2), source.at),
                (source.right, range(2), source.at),
            ]
        if unit.kind == "s1":
            tiles = [0] if source.narrow else range(2)
            return [(source.main, range(2), source.at), (source.edge, tiles, source.edge_at)]
        last = source.tiles - 1
        return [
            (source.main, range(source.tiles), source.at),
            (source.edge, [last], source.edge_at),
        ]

    def rows_of(self, unit, part, m, d, first, count):
        ref, tiles, at = part
        pieces = []
        for tile in tiles:
            if unit.kind == "s2":
                rows = [ref[at(m, tile, 2 * (first + q) + d - 1)] for q in range(count)]
                pieces.append(rows[0] if count == 1 else jnp.concatenate(rows, axis=0))
            else:
                shift = d - 1 if unit.kind == "s1" else 0
                pieces.append(
                    ref[pl.ds(at(m, tile, first + shift), count)].reshape(count * self.rows, LANES)
                )
        return pieces

    def conv(self, m, unit):
        r = self.refs
        source = self.maps[unit.source]
        target = getattr(r, "T" + unit.name)
        z = getattr(r, "z" + unit.name)
        planes, tiles, depth = unit.planes, unit.tiles, unit.depth
        chunk = min(planes, 4 if tiles <= 2 else 2)
        lanes = tiles * LANES

        def body(step, sums):
            first = step * chunk
            pieces = []
            for d in range(depth):
                for part in self.parts(unit, source):
                    pieces += self.rows_of(unit, part, m, d, first, chunk)
            left = jnp.concatenate(pieces, axis=1)
            right = target[pl.ds(m * depth, depth), 0 : unit.rows, 0:lanes]
            right = right.reshape(depth * unit.rows, lanes)
            result = lax.dot_general(left, right, DOWN, preferred_element_type=jnp.float32)
            for tile in range(tiles):
                block = result[:, tile * LANES : (tile + 1) * LANES]
                z[pl.ds(m * tiles * planes + tile * planes + first, chunk)] = block.reshape(
                    chunk, self.rows, LANES
                )
            return (sums[0] + partial_sum(result), sums[1] + partial_sum(result * result))

        zero = jnp.zeros((8, lanes), jnp.float32)
        sums = planes_sum(planes // chunk, body, (zero, zero), 2)
        for seg in unit.segs:
            scale = self.per_cell(unit, seg)
            totals = self.fold(seg, sums)
            self.norm_rows(m, unit, seg, totals, scale)

    def per_cell(self, unit, seg):
        blocks = seg.tiles * LANES // seg.cout
        small, large = self.cells
        count = unit.planes * blocks
        return jnp.where(self.core == 0, 1.0 / (large * count), 1.0 / (small * count)).astype(
            jnp.float32
        )

    def fold(self, seg, sums):
        first = seg.tile
        found = []
        for value in sums:
            tiles = [
                value[:, (first + t) * LANES : (first + t + 1) * LANES] for t in range(seg.tiles)
            ]
            if seg.cout <= LANES:
                total = tiles[0]
                for tile in tiles[1:]:
                    total = total + tile
                total = jnp.sum(self.spread(total, seg.cout), axis=0, keepdims=True)
                found.append([total] * seg.tiles)
            else:
                found.append([jnp.sum(tile, axis=0, keepdims=True) for tile in tiles])
        return found

    def table_row(self, ref, m, seg, tile):
        slot = seg.slot
        if seg.cout > LANES:
            return ref[m, slot : slot + 1, tile * LANES : (tile + 1) * LANES]
        row = jnp.broadcast_to(ref[m, slot : slot + 1, 0:LANES], (8, LANES))
        if seg.cout < LANES:
            row = self.spread(self.keep(row, seg.cout, [0]), seg.cout)
        return row[0:1]

    def norm_rows(self, m, unit, seg, totals, scale):
        st = self.refs.st
        for tile in range(seg.tiles):
            average = totals[0][tile] * scale
            variance = totals[1][tile] * scale - average * average
            inverse = lax.rsqrt(variance + EPS)
            where = m * STATS + unit.stat + seg.tile + tile
            factor = st[where, 4:5] * inverse
            st[where, 0:1] = average
            st[where, 1:2] = inverse
            st[where, 2:3] = factor
            st[where, 3:4] = st[where, 5:6] - average * factor

    def spread_tables(self, m, unit, seg):
        st = self.refs.st
        for tile in range(seg.tiles):
            where = m * STATS + unit.stat + seg.tile + tile
            st[where, 4:5] = self.table_row(self.refs.gains, m, seg, tile)
            st[where, 5:6] = self.table_row(self.refs.shifts, m, seg, tile)

    def normed(self, m, unit, tile, plane):
        st = self.refs.st
        z = getattr(self.refs, "z" + unit.name)
        where = m * STATS + unit.stat + tile
        value = z[m * unit.tiles * unit.planes + tile * unit.planes + plane]
        return value * st[where, 2:3] + st[where, 3:4]

    def apply_a(self, m):
        unit, u = self.units["a"], self.maps["u"]

        def body(plane):
            for tile in range(2):
                value = silu_of(self.normed(m, unit, tile, plane)) * self.masks[0]
                u.store(m, tile, plane, value)

        planes_loop(self.planes, body, TURNS)

    def apply_b(self, m):
        unit, top = self.units["b"], self.maps["t"]
        hf, s = self.refs.hf, self.refs.s

        def body(plane):
            for tile in range(2):
                where = m * 2 * self.planes + tile * self.planes + plane
                value = silu_of(self.normed(m, unit, tile, plane) + hf[where]) * self.masks[0]
                s[where] = value
                top.store(m, tile, plane, value)

        planes_loop(self.planes, body, TURNS)

    def apply_rest(self, m, unit):
        sb = self.refs.sb
        for seg in unit.segs:
            chain = self.maps[seg.chain] if seg.chain else None

            def body(plane):
                for tile in range(seg.tiles):
                    value = self.normed(m, unit, seg.tile + tile, plane)
                    if chain is not None:
                        chain.store(m, tile, plane, silu_of(value) * self.masks[0])
                    else:
                        at = message_slot(self.k, seg.dest) + tile * unit.planes + plane
                        sb[at] = value.astype(jnp.bfloat16)

            planes_loop(unit.planes, body, TURNS)
            if chain is None:
                self.message(m, seg.dest).start()

    def message(self, e, other):
        count = 2 * (8 >> max(self.k, other))
        r = self.refs
        return pltpu.make_async_remote_copy(
            src_ref=r.sb.at[pl.ds(message_slot(self.k, other), count)],
            dst_ref=r.rb.at[pl.ds(e * 16 + message_slot(other, self.k), count)],
            send_sem=r.ssem.at[e * 4 + other],
            recv_sem=r.rsem.at[e * 4 + self.k],
            device_id=dict(branch=other),
            device_id_type=pl.DeviceIdType.MESH,
        )

    def arrived(self, e, other):
        count = 2 * (8 >> max(self.k, other))
        r = self.refs
        at = message_slot(self.k, other)
        return pltpu.make_async_remote_copy(
            src_ref=r.sb.at[pl.ds(at, count)],
            dst_ref=r.rb.at[pl.ds(e * 16 + at, count)],
            send_sem=r.ssem.at[e * 4 + other],
            recv_sem=r.rsem.at[e * 4 + other],
            device_id=dict(branch=other),
            device_id_type=pl.DeviceIdType.MESH,
        )

    def others(self):
        return [other for other in range(4) if other != self.k]

    def sent(self, e):
        for other in self.others():
            self.message(e, other).wait_send()

    def receive(self, m):
        r = self.refs
        s, rb, hf, out = r.s, r.rb, r.hf, r.outs
        h = self.maps["h"]

        def total_at(tile, plane):
            where = m * 2 * self.planes + tile * self.planes + plane
            total = s[where]
            for other in self.others():
                count = 8 >> max(self.k, other)
                at = plane >> max(0, other - self.k)
                slot = m * 16 + message_slot(self.k, other) + tile * count + at
                total = total + rb[slot].astype(jnp.float32)
            s[where] = total
            return silu_of(total) * self.masks[0]

        def onward(plane):
            for tile in range(2):
                value = total_at(tile, plane)
                hf[(2 + tile) * self.planes + plane] = value
                h.store(1, tile, plane, value)

        def finish(plane):
            for tile in range(2):
                out[tile * self.planes + plane] = total_at(tile, plane).astype(jnp.bfloat16)

        @pl.when(m + 1 < MODULES)
        def _():
            planes_loop(self.planes, onward, TURNS)

        @pl.when(m + 1 == MODULES)
        def _():
            planes_loop(self.planes, finish, TURNS)

    def take_feature(self, tile, plane, value):
        self.refs.hf[tile * self.planes + plane] = value
        self.maps["h"].store(0, tile, plane, value)

    def take_cotangent(self, tile, plane, value):
        self.refs.gin[tile * self.planes + plane] = value

    def member(self, kind, order):
        kinds = self.refs.kinds
        found, before = jnp.int32(0), jnp.int32(0)
        for at in range(self.count):
            same = kinds[at] == kind
            found = jnp.where(same & (before == order), at, found)
            before = before + same.astype(jnp.int32)
        return found

    def order(self, device):
        kinds = self.refs.kinds
        kind = kinds[device]
        before = jnp.int32(0)
        for at in range(self.count):
            before = before + ((kinds[at] == kind) & (at < device)).astype(jnp.int32)
        return before

    def unpack(self, t, consume):
        r = self.refs
        work, rows, planes = r.work, self.rows, self.planes
        full = SH * SW * C0 // LANES
        gath = r.gathc if t else r.gathx

        @pl.when(self.core == 0)
        def _():
            for at in range(self.large):
                block = gath[self.member(1, at)]
                work[at * ROWS : (at + 1) * ROWS] = block.astype(jnp.float32)

        @pl.when(self.core == 1)
        def _():
            for at in range(self.small):
                block = gath[self.member(0, at), 0:full]
                work[at * full : (at + 1) * full] = block.astype(jnp.float32)
            work[self.small * full : self.large * ROWS] = jnp.zeros(
                (self.large * ROWS - self.small * full, LANES), jnp.float32
            )

        deep = self.large * ROWS // 2
        right = jnp.concatenate([work[pl.ds(j, deep, stride=2)] for j in range(2)], axis=1)
        right = right.astype(jnp.bfloat16)
        cells = Cells(self.core, (rows, LANES), self.small, self.large)
        base = cells.crop * cells.pick(ROWS // 2, full // 2)
        base = base + cells.along * (planes * cells.wide) + cells.across
        base = jnp.where(cells.valid, base, -(1 << 20))
        lane = lax.broadcasted_iota(jnp.int32, (rows, LANES), 1)
        chunk = min(planes, 4)

        def body(step):
            pieces = []
            for q in range(chunk):
                goal = base + (step * chunk + q) * cells.wide
                pieces.append(one_hot(goal, lane, deep))
            left = pieces[0] if chunk == 1 else jnp.concatenate(pieces, axis=0)
            result = lax.dot_general(left, right, DOWN, preferred_element_type=jnp.float32)
            for q in range(chunk):
                for tile in range(2):
                    value = result[q * rows : (q + 1) * rows, tile * LANES : (tile + 1) * LANES]
                    consume(tile, step * chunk + q, value)

        planes_loop(planes // chunk, body)

    def pack_size(self):
        return 48 * self.planes, -(-self.planes * self.rows // LANES) * LANES

    def plan_pack(self):
        r = self.refs
        high, deep = self.pack_size()
        planes = self.planes
        q = lax.broadcasted_iota(jnp.int32, (high, LANES), 0)
        lane = lax.broadcasted_iota(jnp.int32, (high, LANES), 1)
        wide, tall = jnp.where(self.core == 0, 6, 3), jnp.where(self.core == 0, 8, 4)
        cell = jnp.where(self.core == 0, (q * 43691) >> 18, (q * 43691) >> 17)
        across = q - cell * wide
        plane = cell & (planes - 1)
        along = cell >> log2(planes)
        base = plane * self.rows + along * wide + across
        base = jnp.where(along < tall, base, -(1 << 20))
        shard = lax.axis_index("crops")
        for at, device in enumerate((shard, shard + 1 - 2 * self.core)):
            goal = base + self.order(device) * (wide * tall)
            r.hot[at, 0:high, 0:deep] = one_hot(goal, lane, deep)

    def pack(self, units, put):
        high, deep = self.pack_size()
        right = jnp.concatenate([units(tile) for tile in range(2)], axis=1)
        short = deep - right.shape[0]
        parts = [right.astype(jnp.bfloat16)]
        if right.dtype == jnp.float32:
            parts.append((right - parts[0].astype(jnp.float32)).astype(jnp.bfloat16))
        if short:
            empty = jnp.zeros((short, 2 * LANES), jnp.bfloat16)
            parts = [jnp.concatenate([part, empty], axis=0) for part in parts]
        for at in range(2):
            total = None
            for part in parts:
                piece = lax.dot_general(
                    self.refs.hot[at, 0:high, 0:deep],
                    part,
                    DOWN,
                    preferred_element_type=jnp.float32,
                )
                total = piece if total is None else total + piece
            for tile in range(2):
                put(at, pl.ds(tile, high, stride=2), total[:, tile * LANES : (tile + 1) * LANES])

    def pack_outputs(self):
        r = self.refs
        high = 2 * self.pack_size()[0]

        def put(at, where, value):
            r.work[pl.ds(at * ROWS + where.start, where.size, stride=2)] = value

        def units(tile):
            block = r.outs[tile * self.planes : (tile + 1) * self.planes]
            return block.reshape(self.planes * self.rows, LANES)

        self.pack(units, put)
        for at in range(2):
            r.blocks[at, 0:high] = r.work[at * ROWS : at * ROWS + high].astype(jnp.bfloat16)
            if high < ROWS:
                r.blocks[at, high:ROWS] = jnp.zeros((ROWS - high, LANES), jnp.bfloat16)

    def pack_gradient(self):
        r = self.refs
        high = 2 * self.pack_size()[0]

        def put(at, where, value):
            r.slopes[at, where] = value

        def units(tile):
            block = r.gin[tile * self.planes : (tile + 1) * self.planes]
            return block.reshape(self.planes * self.rows, LANES)

        self.pack(units, put)
        if high < ROWS:
            for at in range(2):
                r.slopes[at, high:ROWS] = jnp.zeros((ROWS - high, LANES), jnp.float32)

    def forward(self, m, gather):
        def also(module, step):
            pl.when(m == module)(lambda: gather.step(1, step))

        self.conv(m, self.units["a"])
        self.apply_a(m)
        self.conv(m, self.units["b"])
        self.apply_b(m)
        also(0, 1)
        also(1, 3)

        @pl.when(m > 0)
        def _():
            self.sent(m - 1)

        for name in ("d", "u", "e", "f", "g"):
            if name in self.units:
                self.conv(m, self.units[name])
                self.apply_rest(m, self.units[name])
        also(0, 2)

        @pl.when(m == MODULES - 1)
        def _():
            gather.collect(1)
            self.unpack(1, self.take_cotangent)

        for other in self.others():
            self.arrived(m, other).wait_recv()
        self.receive(m)


    def send_back(self, m):
        r = self.refs
        s, gin, gt, sb = r.s, r.gin, r.gt, r.sb
        e = MODULES + m

        def body(plane):
            for tile in range(2):
                at = tile * self.planes + plane
                value = gin[at] * slope_of(s[m * 2 * self.planes + at])
                gt[at] = value
                for other in range(self.k):
                    sb[message_slot(self.k, other) + at] = value.astype(jnp.bfloat16)

        planes_loop(self.planes, body, TURNS)
        for other in reversed(self.others()):
            if other > self.k:
                count = 8 >> other
                wide = 1 << (other - self.k)

                def pool(plane):
                    for tile in range(2):
                        total = gt[tile * self.planes + plane * wide]
                        for step in range(1, wide):
                            total = total + gt[tile * self.planes + plane * wide + step]
                        slot = message_slot(self.k, other) + tile * count + plane
                        sb[slot] = total.astype(jnp.bfloat16)

                planes_loop(count, pool, TURNS)
            self.message(e, other).start()

    def back_unit(self, m, unit):
        r = self.refs
        st, dyb, z = r.st, r.dyb, getattr(r, "z" + unit.name)
        name, planes, tiles = unit.name, unit.planes, unit.tiles
        e = MODULES + m
        sums = {}

        def upstream(seg, tile, plane, normed):
            at = tile * planes + plane
            if name == "b":
                hf = r.hf[m * 2 * planes + at]
                value = r.gt[at] * slope_of(normed + hf)
                r.gin[at] = value
                return value
            if name == "a":
                return r.gu[at] * slope_of(normed)
            if seg.chain:
                return self.grads[seg.chain][at] * slope_of(normed)
            return r.rb[e * 16 + message_slot(self.k, seg.dest) + at].astype(jnp.float32)

        for seg in unit.segs:

            def body(plane, carry):
                result = []
                for tile in range(seg.tiles):
                    at = (seg.tile + tile) * planes + plane
                    where = m * STATS + unit.stat + seg.tile + tile
                    value = z[m * tiles * planes + at]
                    normed = value * st[where, 2:3] + st[where, 3:4]
                    dy = upstream(seg, tile, plane, normed)
                    dyb[at] = dy
                    zhat = (value - st[where, 0:1]) * st[where, 1:2]
                    result.append(carry[2 * tile] + partial_sum(dy))
                    result.append(carry[2 * tile + 1] + partial_sum(dy * zhat))
                return tuple(result)

            zero = jnp.zeros((8, LANES), jnp.float32)
            found = planes_sum(planes, body, (zero,) * (2 * seg.tiles), TURNS)
            pair = [
                jnp.concatenate([found[2 * tile + which] for tile in range(seg.tiles)], axis=1)
                for which in range(2)
            ]
            plain = SimpleNamespace(**vars(seg))
            plain.tile = 0
            totals = self.fold(plain, pair)
            self.table_grads(m, seg, totals)
            sums[seg.slot] = totals
        dz = self.dz_planes(unit)
        for seg in unit.segs:
            scale = self.per_cell(unit, seg)
            totals = sums[seg.slot]

            def apply(plane):
                for tile in range(seg.tiles):
                    at = (seg.tile + tile) * planes + plane
                    where = m * STATS + unit.stat + seg.tile + tile
                    zhat = (z[m * tiles * planes + at] - st[where, 0:1]) * st[where, 1:2]
                    inner = dyb[at] - totals[0][tile] * scale - zhat * (totals[1][tile] * scale)
                    dz.store(0, seg.tile + tile, plane, inner * st[where, 2:3] * self.masks[0])

            planes_loop(planes, apply, TURNS)
        self.back_data(m, unit, dz)
        first = min(seg.off for seg in unit.segs)
        last = max(seg.off + seg.taps**2 * seg.cin * seg.cout // LANES for seg in unit.segs)
        wanted = (self.quarter * self.share < last) & ((self.quarter + 1) * self.share > first)

        @pl.when(wanted)
        def _():
            self.back_kernel(m, unit, dz)

    def dz_planes(self, unit):
        r = self.refs
        mode = {"p1": "p", "s2": "dz2", "s1": "wide" if self.k == 3 else "s1"}[unit.kind]
        return Planes(
            mode,
            unit.tiles,
            unit.planes,
            self.masks,
            self.rows,
            r.dC,
            r.dE,
            r.dR,
            self.k <= 1 and unit.kind == "s1",
        )

    def table_grads(self, m, seg, totals):
        gg = self.refs.gg
        slot = seg.slot
        for which, found in ((0, totals[1]), (1, totals[0])):
            if seg.cout > LANES:
                for tile in range(2):
                    gg[m, which, slot : slot + 1, tile * LANES : (tile + 1) * LANES] = found[tile]
            else:
                row = jnp.broadcast_to(found[0], (8, LANES))
                if seg.cout < LANES:
                    row = self.keep(row, seg.cout, [0])
                gg[m, which, slot : slot + 1, 0:LANES] = row[0:1]

    def wide_rows(self, ref, at, tiles, plane, count):
        pieces = [
            ref[pl.ds(at(0, tile, plane), count)].reshape(count * self.rows, LANES)
            for tile in range(tiles)
        ]
        return pieces[0] if tiles == 1 else jnp.concatenate(pieces, axis=1)

    def back_data(self, m, unit, dz):
        r = self.refs
        kind, tiles = unit.kind, unit.tiles
        target = getattr(r, "T" + unit.name)
        lanes = tiles * LANES
        rows = self.rows

        def kernel_rows(d, first, count):
            return target[m * unit.depth + d, first : first + count, 0:lanes]

        def product(left, right):
            return lax.dot_general(left, right, ACROSS, preferred_element_type=jnp.float32)

        def put(ref, tile, planes, first, count, value, step=1, add=False):
            block = value.reshape(count, rows, LANES)
            for q in range(count):
                at = tile * planes + first + q * step
                ref[at] = ref[at] + block[q] if add else block[q]

        planes = unit.planes
        if kind == "s1":
            goal = r.gu if unit.name == "b" else r.gin
            add = unit.name == "a"
            chunk = min(planes, 4)
            across = getattr(r, "T" + unit.name + unit.name)

            def body(step):
                first = step * chunk
                if self.k == 3:
                    total = None
                    for d in range(3):
                        for ref, at in ((dz.right, 0), (dz.main, 256), (dz.edge, 512)):
                            left = self.wide_rows(ref, dz.at, 2, first + 1 - d, chunk)
                            piece = product(left, kernel_rows(d, at, 256))
                            total = piece if total is None else total + piece
                else:
                    narrow = 1 if dz.narrow else 2
                    left = []
                    for d in range(3):
                        at = first + 1 - d
                        left.append(self.wide_rows(dz.main, dz.at, 2, at, chunk))
                        left.append(self.wide_rows(dz.edge, dz.edge_at, narrow, at, chunk))
                    right = across[pl.ds(m * 3, 3), 0 : unit.rows].reshape(3 * unit.rows, 256)
                    total = lax.dot_general(
                        jnp.concatenate(left, axis=1),
                        right,
                        DOWN,
                        preferred_element_type=jnp.float32,
                    )
                for tile in range(2):
                    put(
                        goal,
                        tile,
                        planes,
                        first,
                        chunk,
                        total[:, tile * LANES : (tile + 1) * LANES],
                        add=add,
                    )

            planes_loop(planes // chunk, body, 2)
            return
        if kind == "p1":
            left = self.wide_rows(dz.main, dz.at, tiles, 0, planes)
            total = product(left, kernel_rows(0, 0, 256))
            for tile in range(2):
                put(
                    r.gt,
                    tile,
                    planes,
                    0,
                    planes,
                    total[:, tile * LANES : (tile + 1) * LANES],
                    add=True,
                )
            return
        goal = self.grads[unit.source]
        add = unit.source == "t"
        lanes_in = unit.lanes_in
        count_in = unit.planes_in
        for parity, terms in ((0, [(1, 0)]), (1, [(2, 0), (0, 1)])):
            total, side = None, None
            for d, offset in terms:
                left = self.wide_rows(dz.main, dz.at, tiles, offset, planes)
                piece = product(left, kernel_rows(d, 0, lanes_in))
                total = piece if total is None else total + piece
                left = self.wide_rows(dz.edge, dz.at, tiles, offset, planes)
                piece = product(left, kernel_rows(d, lanes_in, LANES))
                side = piece if side is None else side + piece
            for tile in range(lanes_in // LANES):
                value = total[:, tile * LANES : (tile + 1) * LANES]
                if tile == lanes_in // LANES - 1:
                    value = value + side
                put(goal, tile, count_in, parity, planes, value, step=2, add=add)

    def back_kernel(self, m, unit, dz):
        r = self.refs
        G, rep, wgv = r.work, r.rep, r.wgv
        tiles, planes = unit.tiles, unit.planes
        source = self.maps[unit.source]
        right = self.wide_rows(dz.main, dz.at, tiles, 0, planes)

        def gather(d):
            at = 0
            for part in self.parts(unit, source):
                pieces = self.rows_of(unit, part, m, d, 0, planes)
                left = pieces[0] if len(pieces) == 1 else jnp.concatenate(pieces, axis=1)
                count = left.shape[1]
                result = lax.dot_general(left, right, ALONG, preferred_element_type=jnp.float32)
                for tile in range(tiles):
                    row = pl.multiple_of((d * tiles + tile) * unit.rows + at, 8)
                    G[pl.ds(row, count)] = result[:, tile * LANES : (tile + 1) * LANES]
                at += count

        if self.k == 3 and unit.kind == "s1":
            self.direct_kernel(m, unit, right)
            return
        planes_loop(unit.depth, gather)
        for seg in unit.segs:
            self.fold_kernel(m, unit, seg)

    def direct_kernel(self, m, unit, right):
        wgv, (seg,) = self.refs.wgv, unit.segs
        source = self.maps[unit.source]
        span = 2 * seg.cin
        low, high = self.quarter * self.share, (self.quarter + 1) * self.share

        def tap_row(d):
            first = seg.off + d * (3 * span)

            @pl.when((first < high) & (first + 3 * span > low))
            def _():
                for column, part in enumerate(self.parts(unit, source)):
                    pieces = self.rows_of(unit, part, m, d, 0, unit.planes)
                    left = jnp.concatenate(pieces, axis=1)
                    result = lax.dot_general(left, right, ALONG, preferred_element_type=jnp.float32)
                    for tile in range(2):
                        rows = pl.ds(first + column * span + tile, seg.cin, stride=2)
                        wgv[rows] = result[:, tile * LANES : (tile + 1) * LANES]

        planes_loop(unit.depth, tap_row)

    def fold_kernel(self, m, unit, seg):
        r = self.refs
        G, rep, wgv = r.work, r.rep, r.wgv
        cin, cout, tiles = seg.cin, seg.cout, unit.tiles
        width = 3 if seg.taps == 3 else 1
        found = links(self.k, unit, seg)
        off = seg.off

        def fold(d):
            for column in range(width):
                tap = d * width + column
                totals = []
                for tile in range(seg.tiles):
                    total = None
                    for row, which, wanted in found:
                        if which != column:
                            continue
                        at = pl.multiple_of((d * tiles + seg.tile + tile) * unit.rows + row, 8)
                        piece = G[pl.ds(at, cin)]
                        if cout <= LANES:
                            local = self.local_blocks(seg, tile, wanted)
                            if not local:
                                continue
                            piece = self.keep(piece, cout, local)
                        total = piece if total is None else total + piece
                    totals.append(total)
                if cout > LANES:
                    for tile in range(2):
                        wgv[pl.ds(off + tap * (2 * cin) + tile, cin, stride=2)] = totals[tile]
                    continue
                total = None
                for piece in totals:
                    if piece is not None:
                        total = piece if total is None else total + piece
                if cout == LANES:
                    wgv[pl.ds(pl.multiple_of(off + tap * cin, 8), cin)] = total
                else:
                    rep[pl.ds(pl.multiple_of(tap * cin, cin), cin)] = self.spread(total, cout)

        planes_loop(unit.depth, fold)
        if cout < LANES:
            ratio = LANES // cout
            count = width * width * cin // ratio
            total = None
            for part in range(ratio):
                piece = self.keep(rep[pl.ds(part, count, stride=ratio)], cout, [part])
                total = piece if total is None else total + piece
            wgv[off : off + count] = total

    def backward(self, m, meanwhile):
        e = MODULES + m
        last = m == MODULES - 1
        self.sent(jnp.where(last, m, e + 1))
        self.send_back(m)
        pl.when(last)(meanwhile)
        for name in ("g", "f", "e", "d", "u"):
            if name in self.units:
                for seg in self.units[name].segs:
                    if seg.dest >= 0:
                        self.arrived(e, seg.dest).wait_recv()
                self.back_unit(m, self.units[name])
        self.back_unit(m, self.units["b"])
        self.back_unit(m, self.units["a"])


STATS = 20
TURNS = 8
NAMES = list(
    dict(x=0, cot=0, w=0, gains=0, shifts=0, kinds=0, out=0, grad=0, wg=0, gain=0, shift=0)
)


def one_hot(goal, lane, deep):
    pieces = [
        jnp.where(goal == lane + first, 1.0, 0.0).astype(jnp.bfloat16)
        for first in range(0, deep, LANES)
    ]
    return jnp.concatenate(pieces, axis=1)


class Cells:
    def __init__(self, core, shape, small, large):
        self.core = core
        row = lax.broadcasted_iota(jnp.int32, shape, 0)
        self.wide = self.pick(LW // 8, SW // 8)
        tall = self.pick(LH // 8, SH // 8)
        self.crop = self.pick((row * 43691) >> 21, (row * 43691) >> 19)
        inner = row - self.crop * (self.wide * tall)
        self.along = self.pick((inner * 43691) >> 18, (inner * 43691) >> 17)
        self.across = inner - self.along * self.wide
        self.valid = self.crop < self.pick(large, small)
        self.last = tall - 1

    def pick(self, large, small):
        return jnp.where(self.core == 0, large, small)


def fill_masks(refs, rows, core, small, large):
    cells = Cells(core, (rows, LANES), small, large)
    valid = cells.valid
    six = cells.wide == 6
    up, down = valid & (cells.along > 0), valid & (cells.along < cells.last)
    tables = (
        valid,
        valid & (cells.across > 0),
        valid & (cells.across < cells.wide - 1),
        up & six,
        up & jnp.logical_not(six),
        down & six,
        down & jnp.logical_not(six),
    )
    for at, table in enumerate(tables):
        refs.masks[at] = jnp.where(table, 1.0, 0.0)


class Gather:
    def __init__(self, refs, core, count):
        self.refs, self.core, self.count = refs, core, count
        self.z = lax.axis_index("crops") // 2
        self.last = count // 2 - 1

    def hop(self, t, source, right):
        r = self.refs
        at = source * 2 + self.core
        gath = r.gathc if t else r.gathx
        to = self.z + 1 if right else self.z - 1
        return pltpu.make_async_remote_copy(
            src_ref=gath.at[at],
            dst_ref=gath.at[at],
            send_sem=r.hsem.at[(t * (self.last + 1) + source) * 3 + (0 if right else 1)],
            recv_sem=r.gsem.at[t * self.count + at],
            device_id=dict(crops=to * 2 + self.core),
            device_id_type=pl.DeviceIdType.MESH,
        )

    def across(self, t, source, core, rows):
        r = self.refs
        at = source * 2 + core
        gath = r.gathc if t else r.gathx
        return pltpu.make_async_remote_copy(
            src_ref=gath.at[at, pl.ds(0, rows)],
            dst_ref=gath.at[at, pl.ds(0, rows)],
            send_sem=r.hsem.at[(t * (self.last + 1) + source) * 3 + 2],
            recv_sem=r.gsem.at[t * self.count + at],
            device_id=dict(crops=self.z * 2 + 1 - self.core),
            device_id_type=pl.DeviceIdType.MESH,
        )

    def each_core(self, action):
        for core, rows in ((0, SH * SW * C0 // LANES), (1, ROWS)):

            @pl.when(self.core == core)
            def _():
                action(core, rows)

    def send(self, t, source, rightward, leftward):
        if rightward:

            @pl.when(self.z < self.last)
            def _():
                self.hop(t, source, True).start()

        if leftward:

            @pl.when(self.z > 0)
            def _():
                self.hop(t, source, False).start()

        self.each_core(lambda core, rows: self.across(t, source, core, rows).start())

    def step(self, t, s):
        r = self.refs
        if s == 0:
            at = self.z * 2 + self.core
            if t:
                r.gathc[at] = r.cot[...]
            else:
                r.gathx[at] = r.x[...]
            self.send(t, self.z, True, True)
            return

        @pl.when(self.z >= s)
        def _():
            self.hop(t, self.z - s, True).wait_recv()
            self.send(t, self.z - s, True, False)

        @pl.when(self.z + s <= self.last)
        def _():
            self.hop(t, self.z + s, True).wait_recv()
            self.send(t, self.z + s, False, True)

    def collect(self, t):
        for source in range(self.last + 1):
            for core, rows in ((0, ROWS), (1, SH * SW * C0 // LANES)):

                @pl.when(self.core == core)
                def _():
                    self.across(t, source, 1 - core, rows).wait_recv()

    def finish(self, t):
        def sent(source, rightward, leftward):
            if rightward:

                @pl.when(self.z < self.last)
                def _():
                    self.hop(t, source, True).wait_send()

            if leftward:

                @pl.when(self.z > 0)
                def _():
                    self.hop(t, source, False).wait_send()

            self.each_core(lambda core, rows: self.across(t, source, core, rows).wait_send())

        sent(self.z, True, True)
        for s in range(1, self.last + 1):

            @pl.when(self.z >= s)
            def _():
                sent(self.z - s, True, False)

            @pl.when(self.z + s <= self.last)
            def _():
                sent(self.z + s, False, True)


def scratch_table(rows, weight_rows, count):
    def half(many):
        return pltpu.VMEM((many, rows, LANES), jnp.bfloat16)

    def full(many):
        return pltpu.VMEM((many, rows, LANES), jnp.float32)

    def expanded(depth, deep, wide):
        return pltpu.VMEM((MODULES * depth, deep, wide), jnp.bfloat16)

    _, span, _ = pair_rows(weight_rows, count)
    return dict(
        masks=full(MASKS),
        hC=half(2 * 20),
        hE=half(2 * 10),
        hR=half(2 * 6),
        uC=half(2 * 20),
        uE=half(2 * 10),
        uR=half(2 * 6),
        tC=half(2 * 18),
        tE=half(2 * 9),
        c1C=half(2 * 5),
        c1E=half(2 * 5),
        c2C=half(2 * 5),
        c2E=half(2 * 5),
        c3C=half(2 * 3),
        c3E=half(2 * 3),
        dC=half(20),
        dE=half(20),
        dR=half(6),
        outs=half(16),
        hf=full(2 * 16),
        s=full(2 * 16),
        za=full(2 * 16),
        zb=full(2 * 16),
        zd=full(2 * 16),
        zu=full(2 * 8),
        ze=full(2 * 4),
        zf=full(2 * 2),
        zg=full(2 * 2),
        gt=full(16),
        gu=full(16),
        gin=full(16),
        gc1=full(4),
        gc2=full(4),
        gc3=full(2),
        dyb=full(16),
        sb=half(16),
        rb=half(4 * 16),
        st=pltpu.VMEM((MODULES * STATS, 8, LANES), jnp.float32),
        Ta=expanded(3, 768, 256),
        Tb=expanded(3, 768, 256),
        Taa=expanded(3, 512, 256),
        Tbb=expanded(3, 512, 256),
        Td=expanded(3, 384, 512),
        Tu=expanded(1, 256, 768),
        Te=expanded(3, 256, 256),
        Tf=expanded(3, 256, 128),
        Tg=expanded(3, 256, 256),
        raw=pltpu.VMEM((9408, LANES), jnp.bfloat16),
        work=pltpu.VMEM((4608, LANES), jnp.float32),
        rep=pltpu.VMEM((640, LANES), jnp.float32),
        wgv=pltpu.VMEM((weight_rows, LANES), jnp.float32),
        wq=pltpu.VMEM((MODULES, 2 * weight_rows // count, LANES), jnp.float32),
        wr=pltpu.VMEM((MODULES, span, LANES), jnp.float32),
        gathx=pltpu.VMEM((count, ROWS, LANES), jnp.bfloat16),
        gathc=pltpu.VMEM((count, ROWS, LANES), jnp.bfloat16),
        hot=pltpu.VMEM((2, 384, 768), jnp.bfloat16),
        blocks=pltpu.VMEM((2, ROWS, LANES), jnp.bfloat16),
        slopes=pltpu.VMEM((2, ROWS, LANES), jnp.float32),
        blockr=pltpu.VMEM((ROWS, LANES), jnp.bfloat16),
        sloper=pltpu.VMEM((ROWS, LANES), jnp.float32),
        gg=pltpu.VMEM((MODULES, 2, SLOTS, 256), jnp.float32),
        ggr=pltpu.VMEM((MODULES, 2, SLOTS, 256), jnp.float32),
        wsem=pltpu.SemaphoreType.DMA((8,)),
        ssem=pltpu.SemaphoreType.DMA((16,)),
        rsem=pltpu.SemaphoreType.DMA((16,)),
        hsem=pltpu.SemaphoreType.DMA((3 * count,)),
        gsem=pltpu.SemaphoreType.DMA((2 * count,)),
        psem=pltpu.SemaphoreType.DMA((5,)),
        qsem=pltpu.SemaphoreType.DMA((5,)),
        osem=pltpu.SemaphoreType.DMA((1,)),
    )


def pair_rows(weight_rows, count):
    share = weight_rows // count
    low = share // 8 * 8
    return share, 2 * share - low, low


def greet(core, count):
    barrier = pltpu.get_barrier_semaphore()
    me, shard = lax.axis_index("branch"), lax.axis_index("crops")
    z = shard // 2

    def signal(**where):
        pl.semaphore_signal(barrier, inc=1, device_id=where, device_id_type=pl.DeviceIdType.MESH)

    for step in range(1, 4):
        signal(branch=lax.rem(me + step, 4))
    signal(crops=shard + 1 - 2 * core)

    @pl.when(z > 0)
    def _():
        signal(crops=shard - 2)

    @pl.when(z < count // 2 - 1)
    def _():
        signal(crops=shard + 2)

    ends = (z == 0).astype(jnp.int32) + (z == count // 2 - 1).astype(jnp.int32)
    pl.semaphore_wait(barrier, 6 - ends)


def whole_kernel(names, rows, large, small, *args):
    refs = SimpleNamespace(**dict(zip(names, args)))
    count = large + small
    me, shard = lax.axis_index("branch"), lax.axis_index("crops")
    core = shard % 2
    weight_rows = refs.wgv.shape[0]
    share, span, low = pair_rows(weight_rows, count)
    quarter = pl.multiple_of(shard // 2 * (2 * share), 8)

    class Lazy:
        def __getitem__(self, index):
            return refs.masks[index]

    def across(source, goal, index):
        return pltpu.make_async_remote_copy(
            src_ref=source,
            dst_ref=goal,
            send_sem=refs.psem.at[index],
            recv_sem=refs.qsem.at[index],
            device_id=dict(crops=shard + 1 - 2 * core),
            device_id_type=pl.DeviceIdType.MESH,
        )

    def kernel_pair(m):
        at = pl.multiple_of(low * (1 - core), 8)
        return across(refs.wq.at[m, pl.ds(at, span)], refs.wr.at[m], m)

    outputs_pair = across(refs.blocks.at[1], refs.blockr, 2)
    gradient_pair = across(refs.slopes.at[1], refs.sloper, 3)
    table_pair = across(refs.gg, refs.ggr, 4)
    gather = Gather(refs, core, count)

    def every(action):
        for k in range(4):

            @pl.when(me == k)
            def _():
                action(Branch(k, rows, large, small, 2 * share, refs, Lazy(), core))

    def begin(branch):
        branch.fetch_first()

    def prepare(branch):
        found = branch.segments()
        stops = {0: 1, min(2, len(found) - 2): 2, len(found) - 1: 3}
        for index, (unit, seg) in enumerate(found):
            branch.expand(index)
            if index in stops:
                gather.step(0, stops[index])

    def main(branch):
        branch.unpack(0, branch.take_feature)
        branch.maps["h"].close(0)
        gather.step(1, 0)

        def ahead(m, carry):
            branch.forward(m, gather)
            return carry

        def meanwhile():
            branch.plan_pack()
            branch.pack_outputs()
            outputs_pair.start()

        def back(step, carry):
            m = MODULES - 1 - step
            branch.backward(m, meanwhile)
            refs.wq[m] = refs.wgv[pl.ds(quarter, 2 * share)]
            kernel_pair(m).start()
            return carry

        lax.fori_loop(0, MODULES, ahead, 0)
        lax.fori_loop(0, MODULES, back, 0)
        branch.sent(MODULES)
        branch.pack_gradient()
        gradient_pair.start()
        table_pair.start()

    every(begin)
    greet(core, count)
    gather.step(0, 0)
    fill_masks(refs, rows, core, small, large)
    refs.wgv[pl.ds(quarter, 2 * share)] = jnp.zeros((2 * share, LANES), jnp.float32)
    refs.gg[...] = jnp.zeros(refs.gg.shape, jnp.float32)
    every(prepare)
    gather.collect(0)
    every(main)

    for step in range(MODULES):
        m = MODULES - 1 - step
        kernel_pair(m).wait()
        mine = refs.wq[m, pl.ds(pl.multiple_of(low * core, 8), span)]
        refs.work[pl.ds(m, span, stride=MODULES)] = mine + refs.wr[m]
    skip = pl.multiple_of(core * (MODULES * (share - low)), 8)
    leave = pltpu.make_async_copy(
        refs.work.at[pl.ds(skip, MODULES * share)], refs.wg, refs.osem.at[0]
    )
    leave.start()
    outputs_pair.wait()
    gradient_pair.wait()
    table_pair.wait()
    own = refs.kinds[shard] != core
    refs.out[...] = jnp.where(own, refs.blocks[0].astype(jnp.float32), refs.blockr[...].astype(jnp.float32)).astype(jnp.bfloat16)
    refs.grad[...] = jnp.where(own, refs.slopes[0], refs.sloper[...])
    width = 256 // count
    for which, goal in ((0, refs.gain), (1, refs.shift)):
        for m in range(MODULES):
            total = refs.gg[m, which] + refs.ggr[m, which]
            found = None
            for at in range(count):
                piece = jnp.where(shard == at, total[:, at * width : (at + 1) * width], 0.0)
                found = piece if found is None else found + piece
            goal[m] = found
    gather.finish(0)
    gather.finish(1)
    leave.wait()


def whole_call(rows, large, small, x, cot, w, gains, shifts, kinds):
    count = large + small
    weight_rows = w.shape[0] // MODULES
    table = scratch_table(rows, weight_rows, count)
    vmem = pl.BlockSpec(memory_space=pltpu.VMEM)
    hbm = pl.BlockSpec(memory_space=pl.ANY)
    smem = pl.BlockSpec(memory_space=pltpu.SMEM)
    tables = jax.ShapeDtypeStruct((MODULES, SLOTS, 256 // count), jnp.float32)
    return pl.pallas_call(
        partial(whole_kernel, NAMES + list(table), rows, large, small),
        out_shape=(
            jax.ShapeDtypeStruct((ROWS, LANES), jnp.bfloat16),
            jax.ShapeDtypeStruct((ROWS, LANES), jnp.float32),
            jax.ShapeDtypeStruct((MODULES * weight_rows // count, LANES), jnp.float32),
            tables,
            tables,
        ),
        in_specs=[vmem, vmem, hbm, vmem, vmem, smem],
        out_specs=(vmem, vmem, hbm, vmem, vmem),
        scratch_shapes=list(table.values()),
        compiler_params=pltpu.CompilerParams(
            collective_id=0, has_side_effects=True, vmem_limit_bytes=62 * 1024 * 1024
        ),
    )(x, cot, w, gains, shifts, kinds)


def leave_kernel(*args):
    sources, goals, rooms, arrive, depart = args[:5], args[5:10], args[10:15], args[15], args[16]
    pieces = []
    for source, goal, room in zip(sources, goals, rooms):
        high = source.shape[0]
        parts = 3 if high % 24 == 0 else 1
        for part in range(parts):
            rows = pl.ds(part * (high // parts), high // parts)
            at = len(pieces)
            pieces.append(
                (
                    pltpu.make_async_copy(source.at[rows], room.at[rows], arrive.at[at]),
                    pltpu.make_async_copy(room.at[rows], goal.at[rows], depart.at[at]),
                )
            )
    for come, _ in pieces:
        come.start()
    for come, go in pieces:
        come.wait()
        go.start()
    for _, go in pieces:
        go.wait()


def leave_call(arrays):
    hbm = pl.BlockSpec(memory_space=pl.ANY)
    return pl.pallas_call(
        leave_kernel,
        out_shape=tuple(jax.ShapeDtypeStruct(array.shape, array.dtype) for array in arrays),
        in_specs=[hbm] * 5,
        out_specs=(hbm,) * 5,
        scratch_shapes=[pltpu.VMEM(array.shape, array.dtype) for array in arrays]
        + [pltpu.SemaphoreType.DMA((16,)), pltpu.SemaphoreType.DMA((16,))],
    )(*arrays)


def on_device_grouped(features, weights, gains, shifts, cotangent, size_group):
    count = lax.axis_size("crops")
    large = count // 4
    weight_rows = weights.shape[2] // LANES
    results = whole_call(
        group_rows(count),
        large,
        count - large,
        features[0],
        cotangent[0],
        weights[0]
        .reshape(MODULES, weight_rows, LANES)
        .transpose(1, 0, 2)
        .reshape(MODULES * weight_rows, LANES),
        gains[0],
        shifts[0],
        size_group,
    )
    out, grad, weight_grad, gain, shift = leave_call(results)
    share = weight_rows // count
    weight_grad = weight_grad.reshape(share, MODULES, LANES).transpose(1, 0, 2)
    weight_grad = with_layout_constraint(weight_grad, Layout((1, 0, 2)))
    return (
        out[None],
        grad[None],
        weight_grad.reshape(1, MODULES, share * LANES),
        gain[None],
        shift[None],
    )


def group_rows(count):
    large = count // 4
    rows = max(large * (LH // 8) * (LW // 8), (count - large) * (SH // 8) * (SW // 8))
    return -(-rows // 16) * 16


def fits(count):
    return count % 8 == 0 and group_rows(count) <= 96


def solution(mesh):
    placed = (
        P("branch", "crops", None),
        P("branch", None, None),
        P("branch", None, None, None),
        P("branch", None, None, None),
        P("branch", "crops", None),
        P(),
    )
    return jax.shard_map(
        on_device_grouped if fits(mesh.shape["crops"]) else on_device,
        mesh=mesh,
        in_specs=placed,
        out_specs=(
            P("branch", "crops", None),
            P("branch", "crops", None),
            P("branch", None, "crops"),
            P("branch", None, None, "crops"),
            P("branch", None, None, "crops"),
        ),
        check_vma=False,
    )
```

profile of v0, /device:TPU:0, one launch (start us, length us, event | category | flops | bytes accessed | tf_op | source)
XLA Modules:
  0.0 78.7 jit_solution(10961375488254453547)
XLA Ops:
  0.6 75.0 %shard_map.101 = (bf16[768,128]{1,0:T(8,128)(2,1)}, f32[768,128]{1,0:T(8,128)}, f32[3336,128]{1,0:T(8,128)}, f32[2,8,32]{2,1,0:T(8,128)}, f32[2,8,32]{2,1,0:T(8,128)}) custom-call(bf16[768,128]{1,0:T(8,128)(2,1)} %bitcast.19, bf16[768,128]{1,0:T(8,128)(2,1)} %bitcast.20, bf16[26688,128]{1,0:T(8,128)(2,1)} %bitcast.18, f32[2,8,256]{2,1,0:T(8,128)} %bitcast.21, ...), custom_call_target="tpu_custom_call" | custom-call | tf_op jit(solution)/shard_map/pallas_call | solution.py:2258
  75.6 2.8 %shard_map.102 = (bf16[768,128]{1,0:T(8,128)(2,1)}, f32[768,128]{1,0:T(8,128)}, f32[3336,128]{1,0:T(8,128)}, f32[2,8,32]{2,1,0:T(8,128)}, f32[2,8,32]{2,1,0:T(8,128)}) custom-call(bf16[768,128]{1,0:T(8,128)(2,1)} %get-tuple-element.15.args_0_, f32[768,128]{1,0:T(8,128)} %get-tuple-element.16.args_1_, f32[3336,128]{1,0:T(8,128)} %get-tuple-element.17.args_2_, ...), custom_call_target="tpu_custom_call" | custom-call | tf_op jit(solution)/shard_map/pallas_call | solution.py:2302
where the time goes:
time: 78.9 us; the launch traced here: 78.7 us
  Pallas kernels  77.8 us (99%)
  between operations  0.86 us (1%)
    pallas_call x1, Pallas kernels, whole_call(): pl.pallas_call(partial(whole_kernel, NAMES + list(table), rows, large, sm...  75 us
    pallas_call x1, Pallas kernels, leave_call(): pl.pallas_call(leave_kernel, out_shape=tuple((jax.ShapeDtypeStruct(array....  2.83 us

commit v1 on v0

--- a/solution.py
+++ b/solution.py
@@ -1487,8 +1487,7 @@
         self.apply_a(m)
         self.conv(m, self.units["b"])
         self.apply_b(m)
-        also(0, 1)
-        also(1, 3)
+        also(1, 2)
 
         @pl.when(m > 0)
         def _():
@@ -1498,7 +1497,8 @@
             if name in self.units:
                 self.conv(m, self.units[name])
                 self.apply_rest(m, self.units[name])
-        also(0, 2)
+        also(0, 1)
+        also(1, 3)
 
         @pl.when(m == MODULES - 1)
         def _():
@@ -2024,7 +2024,7 @@
     def expanded(depth, deep, wide):
         return pltpu.VMEM((MODULES * depth, deep, wide), jnp.bfloat16)
 
-    _, span, _ = pair_rows(weight_rows, count)
+    _, span, low = pair_rows(weight_rows, count)
     return dict(
         masks=full(MASKS),
         hC=half(2 * 20),
@@ -2077,15 +2077,17 @@
         work=pltpu.VMEM((4608, LANES), jnp.float32),
         rep=pltpu.VMEM((640, LANES), jnp.float32),
         wgv=pltpu.VMEM((weight_rows, LANES), jnp.float32),
-        wq=pltpu.VMEM((MODULES, 2 * weight_rows // count, LANES), jnp.float32),
-        wr=pltpu.VMEM((MODULES, span, LANES), jnp.float32),
+        wq=pltpu.VMEM((MODULES, low + span, LANES), jnp.float32),
+        wh=pltpu.VMEM((MODULES, low + span, LANES), jnp.bfloat16),
+        wr=pltpu.VMEM((MODULES, span, LANES), jnp.bfloat16),
         gathx=pltpu.VMEM((count, ROWS, LANES), jnp.bfloat16),
         gathc=pltpu.VMEM((count, ROWS, LANES), jnp.bfloat16),
         hot=pltpu.VMEM((2, 384, 768), jnp.bfloat16),
         blocks=pltpu.VMEM((2, ROWS, LANES), jnp.bfloat16),
         slopes=pltpu.VMEM((2, ROWS, LANES), jnp.float32),
         blockr=pltpu.VMEM((ROWS, LANES), jnp.bfloat16),
-        sloper=pltpu.VMEM((ROWS, LANES), jnp.float32),
+        slopeh=pltpu.VMEM((ROWS, LANES), jnp.bfloat16),
+        sloper=pltpu.VMEM((ROWS, LANES), jnp.bfloat16),
         gg=pltpu.VMEM((MODULES, 2, SLOTS, 256), jnp.float32),
         ggr=pltpu.VMEM((MODULES, 2, SLOTS, 256), jnp.float32),
         wsem=pltpu.SemaphoreType.DMA((8,)),
@@ -2101,8 +2103,8 @@
 
 def pair_rows(weight_rows, count):
     share = weight_rows // count
-    low = share // 8 * 8
-    return share, 2 * share - low, low
+    low = share // 16 * 16
+    return share, -(-(2 * share - low) // 16) * 16, low
 
 
 def greet(core, count):
@@ -2153,11 +2155,11 @@
         )
 
     def kernel_pair(m):
-        at = pl.multiple_of(low * (1 - core), 8)
-        return across(refs.wq.at[m, pl.ds(at, span)], refs.wr.at[m], m)
+        at = pl.multiple_of(low * (1 - core), 16)
+        return across(refs.wh.at[m, pl.ds(at, span)], refs.wr.at[m], m)
 
     outputs_pair = across(refs.blocks.at[1], refs.blockr, 2)
-    gradient_pair = across(refs.slopes.at[1], refs.sloper, 3)
+    gradient_pair = across(refs.slopeh, refs.sloper, 3)
     table_pair = across(refs.gg, refs.ggr, 4)
     gather = Gather(refs, core, count)
 
@@ -2196,7 +2198,10 @@
         def back(step, carry):
             m = MODULES - 1 - step
             branch.backward(m, meanwhile)
-            refs.wq[m] = refs.wgv[pl.ds(quarter, 2 * share)]
+            found = refs.wgv[pl.ds(quarter, 2 * share)]
+            refs.wq[m, 0 : 2 * share] = found
+            spare = jnp.zeros((low + span - 2 * share, LANES), jnp.float32)
+            refs.wh[m] = jnp.concatenate([found, spare], axis=0).astype(jnp.bfloat16)
             kernel_pair(m).start()
             return carry
 
@@ -2204,6 +2209,7 @@
         lax.fori_loop(0, MODULES, back, 0)
         branch.sent(MODULES)
         branch.pack_gradient()
+        refs.slopeh[...] = refs.slopes[1].astype(jnp.bfloat16)
         gradient_pair.start()
         table_pair.start()
 
@@ -2221,7 +2227,7 @@
         m = MODULES - 1 - step
         kernel_pair(m).wait()
         mine = refs.wq[m, pl.ds(pl.multiple_of(low * core, 8), span)]
-        refs.work[pl.ds(m, span, stride=MODULES)] = mine + refs.wr[m]
+        refs.work[pl.ds(m, span, stride=MODULES)] = mine + refs.wr[m].astype(jnp.float32)
     skip = pl.multiple_of(core * (MODULES * (share - low)), 8)
     leave = pltpu.make_async_copy(
         refs.work.at[pl.ds(skip, MODULES * share)], refs.wg, refs.osem.at[0]
@@ -2232,7 +2238,7 @@
     table_pair.wait()
     own = refs.kinds[shard] != core
     refs.out[...] = jnp.where(own, refs.blocks[0].astype(jnp.float32), refs.blockr[...].astype(jnp.float32)).astype(jnp.bfloat16)
-    refs.grad[...] = jnp.where(own, refs.slopes[0], refs.sloper[...])
+    refs.grad[...] = jnp.where(own, refs.slopes[0], refs.sloper[...].astype(jnp.float32))
     width = 256 // count
     for which, goal in ((0, refs.gain), (1, refs.shift)):
         for m in range(MODULES):

time: 78.9 us -> 77.1 us (0.977)
  Pallas kernels: 77.8 us -> 76 us
    pallas_call x1, Pallas kernels: 75 us -> 73.2 us  [whole_call(): pl.pallas_call(partial(whole_kernel, NAMES + list(table), rows, large, sm...]
where the time goes in v1:
time: 77.1 us; the launch traced here: 76.9 us
  Pallas kernels  76 us (99%)
  between operations  0.86 us (1%)
    pallas_call x1, Pallas kernels, whole_call(): pl.pallas_call(partial(whole_kernel, NAMES + list(table), rows, large, sm...  73.2 us
    pallas_call x1, Pallas kernels, leave_call(): pl.pallas_call(leave_kernel, out_shape=tuple((jax.ShapeDtypeStruct(array....  2.83 us

profile of v1, /device:TPU:0, one launch (start us, length us, event | category | flops | bytes accessed | tf_op | source)
XLA Modules:
  0.0 76.9 jit_solution(17668605133568079494)
XLA Ops:
  0.6 73.2 %shard_map.101 = (bf16[768,128]{1,0:T(8,128)(2,1)}, f32[768,128]{1,0:T(8,128)}, f32[3336,128]{1,0:T(8,128)}, f32[2,8,32]{2,1,0:T(8,128)}, f32[2,8,32]{2,1,0:T(8,128)}) custom-call(bf16[768,128]{1,0:T(8,128)(2,1)} %bitcast.19, bf16[768,128]{1,0:T(8,128)(2,1)} %bitcast.20, bf16[26688,128]{1,0:T(8,128)(2,1)} %bitcast.18, f32[2,8,256]{2,1,0:T(8,128)} %bitcast.21, ...), custom_call_target="tpu_custom_call" | custom-call | tf_op jit(solution)/shard_map/pallas_call | solution.py:2264
  73.8 2.8 %shard_map.102 = (bf16[768,128]{1,0:T(8,128)(2,1)}, f32[768,128]{1,0:T(8,128)}, f32[3336,128]{1,0:T(8,128)}, f32[2,8,32]{2,1,0:T(8,128)}, f32[2,8,32]{2,1,0:T(8,128)}) custom-call(bf16[768,128]{1,0:T(8,128)(2,1)} %get-tuple-element.15.args_0_, f32[768,128]{1,0:T(8,128)} %get-tuple-element.16.args_1_, f32[3336,128]{1,0:T(8,128)} %get-tuple-element.17.args_2_, ...), custom_call_target="tpu_custom_call" | custom-call | tf_op jit(solution)/shard_map/pallas_call | solution.py:2308

commit v2 on v1

--- a/solution.py
+++ b/solution.py
@@ -1423,7 +1423,7 @@
             goal = base + self.order(device) * (wide * tall)
             r.hot[at, 0:high, 0:deep] = one_hot(goal, lane, deep)
 
-    def pack(self, units, put):
+    def pack(self, units, put, after=None):
         high, deep = self.pack_size()
         right = jnp.concatenate([units(tile) for tile in range(2)], axis=1)
         short = deep - right.shape[0]
@@ -1433,7 +1433,7 @@
         if short:
             empty = jnp.zeros((short, 2 * LANES), jnp.bfloat16)
             parts = [jnp.concatenate([part, empty], axis=0) for part in parts]
-        for at in range(2):
+        for at in (1, 0):
             total = None
             for part in parts:
                 piece = lax.dot_general(
@@ -1445,6 +1445,8 @@
                 total = piece if total is None else total + piece
             for tile in range(2):
                 put(at, pl.ds(tile, high, stride=2), total[:, tile * LANES : (tile + 1) * LANES])
+            if at and after is not None:
+                after()
 
     def pack_outputs(self):
         r = self.refs
@@ -1463,7 +1465,7 @@
             if high < ROWS:
                 r.blocks[at, high:ROWS] = jnp.zeros((ROWS - high, LANES), jnp.bfloat16)
 
-    def pack_gradient(self):
+    def pack_gradient(self, after):
         r = self.refs
         high = 2 * self.pack_size()[0]
 
@@ -1474,10 +1476,10 @@
             block = r.gin[tile * self.planes : (tile + 1) * self.planes]
             return block.reshape(self.planes * self.rows, LANES)
 
-        self.pack(units, put)
         if high < ROWS:
             for at in range(2):
                 r.slopes[at, high:ROWS] = jnp.zeros((ROWS - high, LANES), jnp.float32)
+        self.pack(units, put, after)
 
     def forward(self, m, gather):
         def also(module, step):
@@ -2175,7 +2177,8 @@
 
     def prepare(branch):
         found = branch.segments()
-        stops = {0: 1, min(2, len(found) - 2): 2, len(found) - 1: 3}
+        first, second = ((1, 4), (1, 3), (0, 2), (0, 1))[branch.k]
+        stops = {first: 1, second: 2, len(found) - 1: 3}
         for index, (unit, seg) in enumerate(found):
             branch.expand(index)
             if index in stops:
@@ -2208,10 +2211,13 @@
         lax.fori_loop(0, MODULES, ahead, 0)
         lax.fori_loop(0, MODULES, back, 0)
         branch.sent(MODULES)
-        branch.pack_gradient()
-        refs.slopeh[...] = refs.slopes[1].astype(jnp.bfloat16)
-        gradient_pair.start()
         table_pair.start()
+
+        def share_gradient():
+            refs.slopeh[...] = refs.slopes[1].astype(jnp.bfloat16)
+            gradient_pair.start()
+
+        branch.pack_gradient(share_gradient)
 
     every(begin)
     greet(core, count)

time: 77.1 us -> 78.3 us (1.016)
  Pallas kernels: 76 us -> 77.3 us
    pallas_call x1, Pallas kernels: 73.2 us -> 74.5 us  [whole_call(): pl.pallas_call(partial(whole_kernel, NAMES + list(table), rows, large, sm...]
where the time goes in v2:
time: 78.3 us; the launch traced here: 78.1 us
  Pallas kernels  77.3 us (99%)
  between operations  0.86 us (1%)
    pallas_call x1, Pallas kernels, whole_call(): pl.pallas_call(partial(whole_kernel, NAMES + list(table), rows, large, sm...  74.5 us
    pallas_call x1, Pallas kernels, leave_call(): pl.pallas_call(leave_kernel, out_shape=tuple((jax.ShapeDtypeStruct(array....  2.83 us

profile of v2, /device:TPU:0, one launch (start us, length us, event | category | flops | bytes accessed | tf_op | source)
XLA Modules:
  0.0 78.1 jit_solution(18077658717101370163)
XLA Ops:
  0.6 74.5 %shard_map.101 = (bf16[768,128]{1,0:T(8,128)(2,1)}, f32[768,128]{1,0:T(8,128)}, f32[3336,128]{1,0:T(8,128)}, f32[2,8,32]{2,1,0:T(8,128)}, f32[2,8,32]{2,1,0:T(8,128)}) custom-call(bf16[768,128]{1,0:T(8,128)(2,1)} %bitcast.19, bf16[768,128]{1,0:T(8,128)(2,1)} %bitcast.20, bf16[26688,128]{1,0:T(8,128)(2,1)} %bitcast.18, f32[2,8,256]{2,1,0:T(8,128)} %bitcast.21, ...), custom_call_target="tpu_custom_call" | custom-call | tf_op jit(solution)/shard_map/pallas_call | solution.py:2270
  75.1 2.8 %shard_map.102 = (bf16[768,128]{1,0:T(8,128)(2,1)}, f32[768,128]{1,0:T(8,128)}, f32[3336,128]{1,0:T(8,128)}, f32[2,8,32]{2,1,0:T(8,128)}, f32[2,8,32]{2,1,0:T(8,128)}) custom-call(bf16[768,128]{1,0:T(8,128)(2,1)} %get-tuple-element.15.args_0_, f32[768,128]{1,0:T(8,128)} %get-tuple-element.16.args_1_, f32[3336,128]{1,0:T(8,128)} %get-tuple-element.17.args_2_, ...), custom_call_target="tpu_custom_call" | custom-call | tf_op jit(solution)/shard_map/pallas_call | solution.py:2314

commit v3 on v2

--- a/solution.py
+++ b/solution.py
@@ -2177,7 +2177,7 @@
 
     def prepare(branch):
         found = branch.segments()
-        first, second = ((1, 4), (1, 3), (0, 2), (0, 1))[branch.k]
+        first, second = ((0, 2), (1, 3), (0, 2), (0, 1))[branch.k]
         stops = {first: 1, second: 2, len(found) - 1: 3}
         for index, (unit, seg) in enumerate(found):
             branch.expand(index)

time: 78.3 us -> 77.7 us (level)
  no operation moved by 1% of the time
where the time goes in v3:
time: 77.7 us; the launch traced here: 77.5 us
  Pallas kernels  76.7 us (99%)
  between operations  0.86 us (1%)
    pallas_call x1, Pallas kernels, whole_call(): pl.pallas_call(partial(whole_kernel, NAMES + list(table), rows, large, sm...  73.9 us
    pallas_call x1, Pallas kernels, leave_call(): pl.pallas_call(leave_kernel, out_shape=tuple((jax.ShapeDtypeStruct(array....  2.83 us

profile of v3, /device:TPU:0, one launch (start us, length us, event | category | flops | bytes accessed | tf_op | source)
XLA Modules:
  0.0 77.5 jit_solution(12321488313029728864)
XLA Ops:
  0.6 73.9 %shard_map.101 = (bf16[768,128]{1,0:T(8,128)(2,1)}, f32[768,128]{1,0:T(8,128)}, f32[3336,128]{1,0:T(8,128)}, f32[2,8,32]{2,1,0:T(8,128)}, f32[2,8,32]{2,1,0:T(8,128)}) custom-call(bf16[768,128]{1,0:T(8,128)(2,1)} %bitcast.19, bf16[768,128]{1,0:T(8,128)(2,1)} %bitcast.20, bf16[26688,128]{1,0:T(8,128)(2,1)} %bitcast.18, f32[2,8,256]{2,1,0:T(8,128)} %bitcast.21, ...), custom_call_target="tpu_custom_call" | custom-call | tf_op jit(solution)/shard_map/pallas_call | solution.py:2270
  74.5 2.8 %shard_map.102 = (bf16[768,128]{1,0:T(8,128)(2,1)}, f32[768,128]{1,0:T(8,128)}, f32[3336,128]{1,0:T(8,128)}, f32[2,8,32]{2,1,0:T(8,128)}, f32[2,8,32]{2,1,0:T(8,128)}) custom-call(bf16[768,128]{1,0:T(8,128)(2,1)} %get-tuple-element.15.args_0_, f32[768,128]{1,0:T(8,128)} %get-tuple-element.16.args_1_, f32[3336,128]{1,0:T(8,128)} %get-tuple-element.17.args_2_, ...), custom_call_target="tpu_custom_call" | custom-call | tf_op jit(solution)/shard_map/pallas_call | solution.py:2314
